TPU v7x, 32 devices: a whole 2x2x4 slice. The times are simulated.
32 devices in a mesh: groups: 2 (over y), row: 4 (over z), col: 4 (over x, core).
Axes of the slice: x: 2, y: 2, z: 4, core: 2. Of those that a mesh axis runs over, the one named last changes fastest.
Arguments:
- currents: float32 [2, 16, 8, 2048], P(None, ('groups', 'row'), 'col'), parts along dimension 1, may hold values from -6 to 6
- library: bfloat16 [32, 64, 128], replicated, may hold values from -0.0546875 to 0.0546875
- block_ids: int32 [16, 8, 25], P(('groups', 'row'), 'col'), parts along dimension 0, may hold values from 0 to 31
- dirs: float32 [2, 2048], replicated, may hold values from -0.7 to 0.7
- beam_dir: int32 [64], P('groups'), parts along dimension 0, may hold values from 0 to 2047
Outputs:
- new_currents: float32 [2, 16, 8, 2048], P(None, ('groups', 'row'), 'col'), parts along dimension 1
- far_pattern: float32 [4096, 64], P(('groups', 'row', 'col')), parts along dimension 0
There are 2 independent parts, one for each index of `groups`. A program takes and returns all parts, laid end to end along the dimension named above; an argument that names none is the same for every part. Nothing has to cross between parts.
All inputs are finite; a program needn't handle non-finite values.
Results may differ from a plain program's by a relative error of at most 0.0065.
Values may be sent and summed in bfloat16 or wider, within the bound.
No kernel may reach another device: no remote copies, remote signals or barrier semaphores. Data moves between devices by JAX's collectives and lax.ppermute only.
A program may use at most 64 MiB of HBM per device.

v0:
```python
import math

import jax
import jax.numpy as jnp
from jax import lax
from jax.sharding import PartitionSpec as P

pi_value = 3.141592653589793
dir_block = 512


def with_halo(cells, sides, width):
    for axis, dim in sides:
        count = lax.axis_size(axis)
        ends = count - 1
        head = lax.slice_in_dim(cells, 0, width, axis=dim)
        tail = lax.slice_in_dim(cells, cells.shape[dim] - width, cells.shape[dim], axis=dim)
        cells = jnp.concatenate(
            [
                lax.ppermute(tail, axis, [(i, (i + 1) % count) for i in range(ends)]),
                cells,
                lax.ppermute(head, axis, [((i + 1) % count, i) for i in range(ends)]),
            ],
            axis=dim,
        )
    return cells


def phases(dir_rows, sub_pos, elem_pos):
    sub_angle = pi_value * (
        dir_rows[0][:, None] * sub_pos[0][None, :] + dir_rows[1][:, None] * sub_pos[1][None, :]
    )
    elem_angle = pi_value * (
        dir_rows[0][:, None] * elem_pos[0][None, :] + dir_rows[1][:, None] * elem_pos[1][None, :]
    )
    sub_cos = jnp.cos(sub_angle)[:, :, None]
    sub_sin = jnp.sin(sub_angle)[:, :, None]
    elem_cos = jnp.cos(elem_angle)[:, None, :]
    elem_sin = jnp.sin(elem_angle)[:, None, :]
    cosine = sub_cos * elem_cos - sub_sin * elem_sin
    sine = sub_sin * elem_cos + sub_cos * elem_sin
    count = dir_rows.shape[1]
    return (
        cosine.reshape(count, -1).astype(jnp.bfloat16),
        (-sine).reshape(count, -1).astype(jnp.bfloat16),
    )


def coupling(padded, id_table, library, adjoint):
    rows_here = padded.shape[1] - 4
    cols_here = padded.shape[2] - 4
    elems = library.shape[1]
    field_view = padded.reshape(2, rows_here + 4, cols_here + 4, elems, -1)
    spec = "rcnji,rcnjb->rcib" if adjoint else "rcnij,rcnjb->rcib"
    out_re = jnp.zeros((rows_here, cols_here, elems, field_view.shape[4]), jnp.float32)
    out_im = jnp.zeros_like(out_re)
    for row_off in range(5):
        sources = []
        chosen = []
        for col_off in range(5):
            slot_index = 5 * row_off + col_off
            if adjoint:
                row_start = 4 - row_off
                col_start = 4 - col_off
                chosen.append(
                    id_table[
                        row_start : row_start + rows_here,
                        col_start : col_start + cols_here,
                        slot_index,
                    ]
                )
            else:
                row_start = row_off
                col_start = col_off
                chosen.append(id_table[:, :, slot_index])
            sources.append(
                field_view[:, row_start : row_start + rows_here, col_start : col_start + cols_here]
            )
        source_stack = jnp.stack(sources, axis=3)
        block_stack = library[jnp.stack(chosen, axis=2)]
        block_re = block_stack[..., :elems]
        block_im = block_stack[..., elems:]
        real_real = jnp.einsum(spec, block_re, source_stack[0], preferred_element_type=jnp.float32)
        real_imag = jnp.einsum(spec, block_re, source_stack[1], preferred_element_type=jnp.float32)
        imag_real = jnp.einsum(spec, block_im, source_stack[0], preferred_element_type=jnp.float32)
        imag_imag = jnp.einsum(spec, block_im, source_stack[1], preferred_element_type=jnp.float32)
        if adjoint:
            out_re = out_re + real_real + imag_imag
            out_im = out_im + real_imag - imag_real
        else:
            out_re = out_re + real_real - imag_imag
            out_im = out_im + real_imag + imag_real
    return jnp.stack([out_re, out_im])


def pattern_term(radiated_cols, dirs, sub_pos, elem_pos, row_count, scale):
    half_cols = radiated_cols.shape[1] // 2

    def one_block(begin_row, block_size):
        dir_rows = lax.dynamic_slice_in_dim(dirs, begin_row, block_size, 1)
        cosine, sine = phases(dir_rows, sub_pos, elem_pos)
        cos_part = jnp.dot(cosine, radiated_cols, preferred_element_type=jnp.float32)
        sin_part = jnp.dot(sine, radiated_cols, preferred_element_type=jnp.float32)
        return jnp.concatenate(
            [
                cos_part[:, :half_cols] - sin_part[:, half_cols:],
                cos_part[:, half_cols:] + sin_part[:, :half_cols],
            ],
            axis=1,
        )

    block_count = row_count // dir_block
    starts = jnp.arange(block_count, dtype=jnp.int32) * dir_block
    stacked = lax.map(lambda begin_row: one_block(begin_row, dir_block), starts)
    pieces = stacked.reshape(block_count * dir_block, 2 * half_cols)
    return pieces * scale


def adjoint_piece(carry, residual_rows, dirs, sub_pos, elem_pos):
    row_count = residual_rows.shape[0]
    dims_spec = (((0,), (0,)), ((), ()))

    def add_block(totals, local_start, block_size):
        piece_rows = lax.dynamic_slice_in_dim(residual_rows, local_start, block_size, 0)
        dir_rows = lax.dynamic_slice_in_dim(dirs, local_start, block_size, 1)
        cosine, sine = phases(dir_rows, sub_pos, elem_pos)
        cos_part = lax.dot_general(
            cosine, piece_rows, dims_spec, preferred_element_type=jnp.float32
        )
        sin_part = lax.dot_general(sine, piece_rows, dims_spec, preferred_element_type=jnp.float32)
        return (totals[0] + cos_part, totals[1] + sin_part)

    block_count = row_count // dir_block
    carry = lax.fori_loop(
        0,
        block_count,
        lambda number, totals: add_block(totals, number * dir_block, dir_block),
        carry,
    )
    return carry


def line_terms(image_pattern, residual, beams):
    products = jnp.sum(image_pattern * residual, axis=0)
    squares = jnp.sum(image_pattern * image_pattern, axis=0)
    return (products[:beams] + products[beams:], squares[:beams] + squares[beams:])


def local(currents, library, block_ids, dirs, beam_dir):
    beams = beam_dir.shape[0]
    rows_here = currents.shape[1]
    cols_here = currents.shape[2]
    packed = currents.shape[3]
    elems = library.shape[1]
    side = math.isqrt(elems)
    local_elems = rows_here * cols_here * elems
    total_rows = rows_here * lax.axis_size("row")
    total_cols = cols_here * lax.axis_size("col")
    all_elems = total_rows * total_cols * elems
    scale = 1.0 / math.sqrt(all_elems)
    amplitude = math.sqrt(all_elems) / 16.0
    dir_total = dirs.shape[1]
    share_rows = dir_total // lax.axis_size(("row", "col"))
    row_ids = (lax.axis_index("row") * rows_here + jnp.arange(rows_here, dtype=jnp.int32))[:, None]
    col_ids = (lax.axis_index("col") * cols_here + jnp.arange(cols_here, dtype=jnp.int32))[None, :]
    sub_x = (col_ids * side + 0 * row_ids).reshape(-1).astype(jnp.float32) - (
        total_cols * side - 1
    ) / 2.0
    sub_y = (row_ids * side + 0 * col_ids).reshape(-1).astype(jnp.float32) - (
        total_rows * side - 1
    ) / 2.0
    elem_ids = jnp.arange(elems, dtype=jnp.int32)
    sub_pos = (sub_x, sub_y)
    elem_pos = ((elem_ids % side).astype(jnp.float32), (elem_ids // side).astype(jnp.float32))
    padded_ids = with_halo(block_ids, (("row", 0), ("col", 1)), 2)

    def radiate(current_field):
        rounded = current_field.astype(jnp.bfloat16)
        padded = with_halo(rounded, (("row", 1), ("col", 2)), 2)
        coupled = coupling(padded, block_ids, library, False)
        total_field = (current_field.reshape(coupled.shape) + coupled).astype(jnp.bfloat16)
        return jnp.concatenate(
            [
                total_field[0].reshape(local_elems, beams),
                total_field[1].reshape(local_elems, beams),
            ],
            axis=1,
        )

    zero_acc = jnp.zeros((local_elems, 2 * beams), jnp.float32)

    def share_pattern(current_field):
        radiated_cols = radiate(current_field)
        return lax.psum_scatter(
            pattern_term(
                radiated_cols,
                dirs,
                sub_pos,
                elem_pos,
                share_rows * lax.axis_size(("row", "col")),
                scale,
            ),
            ("row", "col"),
            scatter_dimension=0,
            tiled=True,
        )

    share = share_pattern(currents)
    dir_ids = lax.axis_index(("row", "col")) * share_rows + jnp.arange(share_rows, dtype=jnp.int32)
    real_part = amplitude * (dir_ids[:, None] == beam_dir[None, :]).astype(jnp.float32)
    target = jnp.concatenate([real_part, jnp.zeros_like(real_part)], axis=1)
    residual = share - target
    totals = adjoint_piece(
        (zero_acc, zero_acc),
        lax.all_gather(residual.astype(jnp.bfloat16), ("row", "col"), axis=0, tiled=True),
        dirs,
        sub_pos,
        elem_pos,
    )
    p_part, q_part = totals
    grad_re = (p_part[:, :beams] + q_part[:, beams:]) * scale
    grad_im = (p_part[:, beams:] - q_part[:, :beams]) * scale
    raw_gradient = jnp.stack(
        [
            grad_re.reshape(rows_here, cols_here, packed),
            grad_im.reshape(rows_here, cols_here, packed),
        ]
    )
    rounded = raw_gradient.astype(jnp.bfloat16)
    padded = with_halo(rounded, (("row", 1), ("col", 2)), 2)
    gradient = raw_gradient + coupling(padded, padded_ids, library, True).reshape(
        raw_gradient.shape
    )
    image_pattern = share_pattern(gradient)
    part_num, part_den = line_terms(image_pattern, residual, beams)
    numerator, denominator = lax.psum((part_num, part_den), ("row", "col"))
    step_size = numerator / (denominator + 1e-06)
    moved = gradient.reshape(2, rows_here, cols_here, elems, beams) * step_size
    currents = currents - moved.reshape(currents.shape)
    share = share - image_pattern * jnp.concatenate([step_size, step_size])
    return (currents, share)


def solution(mesh):
    return jax.shard_map(
        local,
        mesh=mesh,
        in_specs=(
            P(None, ("groups", "row"), "col", None),
            P(),
            P(("groups", "row"), "col", None),
            P(),
            P("groups"),
        ),
        out_specs=(P(None, ("groups", "row"), "col", None), P(("groups", "row", "col"), None)),
        check_vma=False,
    )
```

profile of v0, /device:TPU:0, one launch (start us, length us, event | category | flops | bytes accessed | tf_op | source)
XLA Modules:
  0.0 424.8 jit_solution(15153616474967476686)
XLA Ops:
  8.1 4.9 %collective-permute-start = (bf16[2,2,2,2048]{3,2,1,0:T(2,128)(2,1)S(1)}, bf16[2,2,2,2048]{3,2,1,0:T(2,128)(2,1)S(1)}, u32[]{:S(2)}, u32[]{:S(2)}) collective-permute-start(bf16[2,2,2,2048]{3,2,1,0:T(2,128)(2,1)S(1)} %convert_element_type.91), channel_id=1, source_target_pairs={{0,4},{4,8},{8,12},{1,5},{5,9},{9,13},{2,6},{6,10},{10,14},{3,7},{... | collective-permute-start | bytes 98312 | tf_op jit(solution)/shard_map/ppermute | solution.py:20
  14.4 4.5 %collective-permute-start.4 = (s32[2,2,25]{2,1,0:T(2,128)}, s32[2,2,25]{2,1,0:T(2,128)S(1)}, u32[]{:S(2)}, u32[]{:S(2)}) collective-permute-start(s32[2,2,25]{2,1,0:T(2,128)} %param.13), channel_id=1, source_target_pairs={{0,4},{4,8},{8,12},{1,5},{5,9},{9,13},{2,6},{6,10},{10,14},{3,7},{... | collective-permute-start | bytes 1208 | tf_op jit(solution)/shard_map/ppermute | solution.py:20
  31.2 3.0 collective-permute-start.7
  36.7 3.0 collective-permute-start.2
  56.1 1.9 convolution_bitcast_fusion.50
  58.0 1.9 convolution_bitcast_fusion.51
  76.4 1.8 convolution_bitcast_fusion.56
  78.2 1.8 convolution_bitcast_fusion.57
  84.8 16.9 %while.38 = (s32[]{:T(128)}, f32[4,512,64]{1,2,0:T(8,128)S(1)}, s32[4]{0:T(128)S(1)}, f32[2,2048]{1,0:T(2,128)S(1)}, bf16[256,64]{1,0:T(8,128)(2,1)S(1)}, /*inde...) while((s32[]{:T(128)}, f32[4,512,64]{1,2,0:T(8,128)S(1)}, ...), condition=%wide.region_1.2_spmd.clone, body=%wide.region_0.1_spmd.clone.sunk | while | flops 34939780 | bytes 2606403 | solution.py:114
  103.4 59.5 %reduce-scatter.3.cloned.1.call-done = f32[128,64]{0,1:T(8,128)} async-done(((f32[2048,64]{0,1:T(8,128)}), f32[128,64]{0,1:T(8,128)}) %reduce-scatter.3.cloned.1.call-update) | async-done | bytes 32784 | tf_op jit(solution)/shard_map/reduce_scatter | solution.py:194
  163.7 20.3 %all_gather.3 = bf16[2048,64]{0,1:T(8,128)(2,1)S(1)} all-gather(bf16[128,64]{0,1:T(8,128)(2,1)S(1)} %fusion.169), channel_id=1, replica_groups=mesh['groups'=2,'row'=4,'col'=4] {'row','col'}, dimensions={0}, use_global_device_ids=true | all-gather | bytes 278528 | tf_op jit(solution)/shard_map/all_gather | solution.py:215
  184.0 6.6 %while.40 = (s32[]{:T(128)}, f32[256,64]{0,1:T(8,128)S(1)}, f32[256,64]{0,1:T(8,128)S(1)}, f32[2,2048]{1,0:T(2,128)S(1)}, bf16[2048,64]{0,1:T(8,128)(2,1)S(1)}, ...) while((s32[]{:T(128)}, f32[256,64]{0,1:T(8,128)S(1)}, ...), condition=%wide.region_4.5_spmd.clone, body=%wide.region_3.4_spmd.clone.sunk | while | flops 34939784 | bytes 2016602 | solution.py:134
  198.8 1.9 collective-permute-start.10
  226.2 1.9 fusion.63
  240.8 1.9 fusion.59
  250.4 4.3 %collective-permute-start.12 = (bf16[2,2,2,2048]{3,2,1,0:T(2,128)(2,1)S(1)}, bf16[2,2,2,2048]{3,2,1,0:T(2,128)(2,1)S(1)}, u32[]{:S(2)}, u32[]{:S(2)}) collective-permute-start(bf16[2,2,2,2048]{3,2,1,0:T(2,128)(2,1)S(1)} %fusion.174), channel_id=1, source_target_pairs={{0,4},{4,8},{8,12},{1,5},{5,9},{9,13},{2,6},{6,10},{10,14},{3,7},{... | collective-permute-start | bytes 98312 | tf_op jit(solution)/shard_map/ppermute | solution.py:20
  256.2 4.2 collective-permute-done.13
  260.6 2.4 collective-permute-start.14
  279.6 1.8 convolution_bitcast_fusion.36
  281.4 1.9 convolution_bitcast_fusion.37
  287.2 1.8 convolution_bitcast_fusion.34
  310.2 16.9 %while.39 = (s32[]{:T(128)}, f32[4,512,64]{1,2,0:T(8,128)S(1)}, s32[4]{0:T(128)S(1)}, f32[2,2048]{1,0:T(2,128)S(1)}, bf16[256,64]{1,0:T(8,128)(2,1)S(1)}, /*inde...) while((s32[]{:T(128)}, f32[4,512,64]{1,2,0:T(8,128)S(1)}, ...), condition=%wide.region_6.7_spmd.clone, body=%wide.region_5.6_spmd.clone.sunk | while | flops 34939780 | bytes 2606403 | solution.py:114
  328.1 56.9 %reduce-scatter.5.cloned.1.call-done = f32[128,64]{0,1:T(8,128)} async-done(((f32[2048,64]{0,1:T(8,128)}), f32[128,64]{0,1:T(8,128)}) %reduce-scatter.5.cloned.1.call-update) | async-done | bytes 32784 | tf_op jit(solution)/shard_map/reduce_scatter | solution.py:194
  386.0 29.6 %all-reduce.1 = (f32[32]{0:T(128)S(1)}, f32[32]{0:T(128)S(1)}) all-reduce(f32[32]{0:T(128)S(1)} %slice_add_fusion.3, f32[32]{0:T(128)S(1)} %slice_add_fusion.2), channel_id=1, replica_groups=mesh['groups'=2,'row'=4,'col'=4] {'row','col'}, use_global_device_ids=true, to_apply=%region_9.10 | all-reduce | flops 64 | bytes 512 | tf_op jit(solution)/shard_map/psum | solution.py:236
  (728 shorter events, 180.5 us)
Async XLA Ops:
  7.2 155.8 %reduce-scatter.3.cloned.1.call-start = ((), (), s32[]{:S(2)}) async-start(), calls=%async_computation.2 | async-start | bytes 557056 | tf_op jit(solution)/shard_map/reduce_scatter | solution.py:194
  8.1 28.4 %collective-permute-start = (bf16[2,2,2,2048]{3,2,1,0:T(2,128)(2,1)S(1)}, bf16[2,2,2,2048]{3,2,1,0:T(2,128)(2,1)S(1)}, u32[]{:S(2)}, u32[]{:S(2)}) collective-permute-start(bf16[2,2,2,2048]{3,2,1,0:T(2,128)(2,1)S(1)} %convert_element_type.91), channel_id=1, source_target_pairs={{0,4},{4,8},{8,12},{1,5},{5,9},{9,13},{2,6},{6,10},{10,14},{3,7},{... | collective-permute-start | bytes 98312 | tf_op jit(solution)/shard_map/ppermute | solution.py:20
  13.1 23.5 %collective-permute-start.1 = (bf16[2,2,2,2048]{3,2,1,0:T(2,128)(2,1)S(1)}, bf16[2,2,2,2048]{3,2,1,0:T(2,128)(2,1)S(1)}, u32[]{:S(2)}, u32[]{:S(2)}) collective-permute-start(bf16[2,2,2,2048]{3,2,1,0:T(2,128)(2,1)S(1)} %convert_element_type.91), channel_id=1, source_target_pairs={{4,0},{8,4},{12,8},{5,1},{9,5},{13,9},{6,2},{10,6},{14,10},{7,3},{... | collective-permute-start | bytes 98312 | tf_op jit(solution)/shard_map/ppermute | solution.py:22
  14.4 15.5 %collective-permute-start.4 = (s32[2,2,25]{2,1,0:T(2,128)}, s32[2,2,25]{2,1,0:T(2,128)S(1)}, u32[]{:S(2)}, u32[]{:S(2)}) collective-permute-start(s32[2,2,25]{2,1,0:T(2,128)} %param.13), channel_id=1, source_target_pairs={{0,4},{4,8},{8,12},{1,5},{5,9},{9,13},{2,6},{6,10},{10,14},{3,7},{... | collective-permute-start | bytes 1208 | tf_op jit(solution)/shard_map/ppermute | solution.py:20
  18.9 11.0 %collective-permute-start.5 = (s32[2,2,25]{2,1,0:T(2,128)}, s32[2,2,25]{2,1,0:T(2,128)S(1)}, u32[]{:S(2)}, u32[]{:S(2)}) collective-permute-start(s32[2,2,25]{2,1,0:T(2,128)} %param.13), channel_id=1, source_target_pairs={{4,0},{8,4},{12,8},{5,1},{9,5},{13,9},{6,2},{10,6},{14,10},{7,3},{... | collective-permute-start | bytes 1208 | tf_op jit(solution)/shard_map/ppermute | solution.py:22
  29.9 5.0 %collective-permute-start.6 = (s32[6,2,25]{2,1,0:T(2,128)S(1)}, s32[6,2,25]{2,1,0:T(2,128)S(1)}, u32[]{:S(2)}, u32[]{:S(2)}) collective-permute-start(s32[6,2,25]{2,1,0:T(2,128)S(1)} %constant_dynamic-update-slice_fusion.32), channel_id=1, source_target_pairs={{1,0},{2,1},{3,2},{5,4},{6,5},{7,6},{9,8},{10,9},{11,10},{13,12},{... | collective-permute-start | bytes 3608 | tf_op jit(solution)/shard_map/ppermute | solution.py:22
  31.2 4.4 %collective-permute-start.7 = (s32[6,2,25]{2,1,0:T(2,128)S(1)}, s32[6,2,25]{2,1,0:T(2,128)S(1)}, u32[]{:S(2)}, u32[]{:S(2)}) collective-permute-start(s32[6,2,25]{2,1,0:T(2,128)S(1)} %constant_dynamic-update-slice_fusion.32), channel_id=1, source_target_pairs={{0,1},{1,2},{2,3},{4,5},{5,6},{6,7},{8,9},{9,10},{10,11},{12,13},{... | collective-permute-start | bytes 3608 | tf_op jit(solution)/shard_map/ppermute | solution.py:20
  36.7 6.9 %collective-permute-start.2 = (bf16[2,6,2,2048]{3,2,1,0:T(2,128)(2,1)S(1)}, bf16[2,6,2,2048]{3,2,1,0:T(2,128)(2,1)S(1)}, u32[]{:S(2)}, u32[]{:S(2)}) collective-permute-start(bf16[2,6,2,2048]{3,2,1,0:T(2,128)(2,1)S(1)} %pad_maximum_fusion.3), channel_id=1, source_target_pairs={{0,1},{1,2},{2,3},{4,5},{5,6},{6,7},{8,9},{9,10},{10,11},{12,13},{... | collective-permute-start | bytes 294920 | tf_op jit(solution)/shard_map/ppermute | solution.py:20
  39.7 4.4 %collective-permute-start.3 = (bf16[2,6,2,2048]{3,2,1,0:T(2,128)(2,1)S(1)}, bf16[2,6,2,2048]{3,2,1,0:T(2,128)(2,1)S(1)}, u32[]{:S(2)}, u32[]{:S(2)}) collective-permute-start(bf16[2,6,2,2048]{3,2,1,0:T(2,128)(2,1)S(1)} %pad_maximum_fusion.3), channel_id=1, source_target_pairs={{1,0},{2,1},{3,2},{5,4},{6,5},{7,6},{9,8},{10,9},{11,10},{13,12},{... | collective-permute-start | bytes 294920 | tf_op jit(solution)/shard_map/ppermute | solution.py:22
  101.8 61.1 %copy-start.65 = (f32[128,32]{0,1:T(8,128)S(1)}, f32[128,32]{0,1:T(8,128)}, u32[]{:S(2)}) copy-start(f32[128,32]{0,1:T(8,128)} %compare_select_fusion) | copy-start | bytes 49156
  102.8 282.2 %reduce-scatter.5.cloned.1.call-start = ((), (), s32[]{:S(2)}) async-start(), calls=%async_computation.3 | async-start | bytes 557056 | tf_op jit(solution)/shard_map/reduce_scatter | solution.py:194
  191.6 6.8 %collective-permute-start.8 = (bf16[2,2,2,2048]{3,2,1,0:T(2,128)(2,1)S(1)}, bf16[2,2,2,2048]{3,2,1,0:T(2,128)(2,1)S(1)}, u32[]{:S(2)}, u32[]{:S(2)}) collective-permute-start(bf16[2,2,2,2048]{3,2,1,0:T(2,128)(2,1)S(1)} %convert_element_type.94), channel_id=1, source_target_pairs={{0,4},{4,8},{8,12},{1,5},{5,9},{9,13},{2,6},{6,10},{10,14},{3,7},{... | collective-permute-start | bytes 98312 | tf_op jit(solution)/shard_map/ppermute | solution.py:20
  192.9 5.8 %collective-permute-start.9 = (bf16[2,2,2,2048]{3,2,1,0:T(2,128)(2,1)S(1)}, bf16[2,2,2,2048]{3,2,1,0:T(2,128)(2,1)S(1)}, u32[]{:S(2)}, u32[]{:S(2)}) collective-permute-start(bf16[2,2,2,2048]{3,2,1,0:T(2,128)(2,1)S(1)} %convert_element_type.94), channel_id=1, source_target_pairs={{4,0},{8,4},{12,8},{5,1},{9,5},{13,9},{6,2},{10,6},{14,10},{7,3},{... | collective-permute-start | bytes 98312 | tf_op jit(solution)/shard_map/ppermute | solution.py:22
  198.8 6.0 %collective-permute-start.10 = (bf16[2,6,2,2048]{3,2,1,0:T(2,128)(2,1)S(1)}, bf16[2,6,2,2048]{3,2,1,0:T(2,128)(2,1)S(1)}, u32[]{:S(2)}, u32[]{:S(2)}) collective-permute-start(bf16[2,6,2,2048]{3,2,1,0:T(2,128)(2,1)S(1)} %pad_maximum_fusion.4), channel_id=1, source_target_pairs={{0,1},{1,2},{2,3},{4,5},{5,6},{6,7},{8,9},{9,10},{10,11},{12,13},{... | collective-permute-start | bytes 294920 | tf_op jit(solution)/shard_map/ppermute | solution.py:20
  200.8 4.0 collective-permute-start.11
  250.4 5.9 %collective-permute-start.12 = (bf16[2,2,2,2048]{3,2,1,0:T(2,128)(2,1)S(1)}, bf16[2,2,2,2048]{3,2,1,0:T(2,128)(2,1)S(1)}, u32[]{:S(2)}, u32[]{:S(2)}) collective-permute-start(bf16[2,2,2,2048]{3,2,1,0:T(2,128)(2,1)S(1)} %fusion.174), channel_id=1, source_target_pairs={{0,4},{4,8},{8,12},{1,5},{5,9},{9,13},{2,6},{6,10},{10,14},{3,7},{... | collective-permute-start | bytes 98312 | tf_op jit(solution)/shard_map/ppermute | solution.py:20
  254.7 5.8 %collective-permute-start.13 = (bf16[2,2,2,2048]{3,2,1,0:T(2,128)(2,1)S(1)}, bf16[2,2,2,2048]{3,2,1,0:T(2,128)(2,1)S(1)}, u32[]{:S(2)}, u32[]{:S(2)}) collective-permute-start(bf16[2,2,2,2048]{3,2,1,0:T(2,128)(2,1)S(1)} %fusion.174), channel_id=1, source_target_pairs={{4,0},{8,4},{12,8},{5,1},{9,5},{13,9},{6,2},{10,6},{14,10},{7,3},{... | collective-permute-start | bytes 98312 | tf_op jit(solution)/shard_map/ppermute | solution.py:22
  260.6 5.4 %collective-permute-start.14 = (bf16[2,6,2,2048]{3,2,1,0:T(2,128)(2,1)S(1)}, bf16[2,6,2,2048]{3,2,1,0:T(2,128)(2,1)S(1)}, u32[]{:S(2)}, u32[]{:S(2)}) collective-permute-start(bf16[2,6,2,2048]{3,2,1,0:T(2,128)(2,1)S(1)} %pad_maximum_fusion.5), channel_id=1, source_target_pairs={{0,1},{1,2},{2,3},{4,5},{5,6},{6,7},{8,9},{9,10},{10,11},{12,13},{... | collective-permute-start | bytes 294920 | tf_op jit(solution)/shard_map/ppermute | solution.py:20
  263.0 4.6 %collective-permute-start.15 = (bf16[2,6,2,2048]{3,2,1,0:T(2,128)(2,1)S(1)}, bf16[2,6,2,2048]{3,2,1,0:T(2,128)(2,1)S(1)}, u32[]{:S(2)}, u32[]{:S(2)}) collective-permute-start(bf16[2,6,2,2048]{3,2,1,0:T(2,128)(2,1)S(1)} %pad_maximum_fusion.5), channel_id=1, source_target_pairs={{1,0},{2,1},{3,2},{5,4},{6,5},{7,6},{9,8},{10,9},{11,10},{13,12},{... | collective-permute-start | bytes 294920 | tf_op jit(solution)/shard_map/ppermute | solution.py:22
  327.1 57.9 %copy-start.57 = (f32[128,64]{0,1:T(8,128)S(1)}, f32[128,64]{0,1:T(8,128)}, u32[]{:S(2)}) copy-start(f32[128,64]{0,1:T(8,128)} %reduce-scatter.3.cloned.1.call-done) | copy-start | bytes 98308
  327.1 57.9 %copy-start.66 = (f32[128,32]{0,1:T(8,128)S(1)}, f32[128,32]{0,1:T(8,128)}, u32[]{:S(2)}) copy-start(f32[128,32]{0,1:T(8,128)} %compare_select_fusion) | copy-start | bytes 49156
  327.1 88.7 %copy-start.1 = (f32[2,2,2,2048]{3,2,1,0:T(2,128)S(1)}, f32[2,2,2,2048]{3,2,1,0:T(2,128)}, u32[]{:S(2)}) copy-start(f32[2,2,2,2048]{3,2,1,0:T(2,128)} %param.11) | copy-start | bytes 196612
  327.1 88.7 %copy-start.50 = (f32[1,2,2,2048]{3,2,1,0:T(2,128)S(1)}, f32[1,2,2,2048]{3,2,1,0:T(2,128)}, u32[]{:S(2)}) copy-start(f32[1,2,2,2048]{3,2,1,0:T(2,128)} %copy-done.49) | copy-start | bytes 98308
  327.1 88.7 %copy-start.52 = (f32[1,2,2,2048]{3,2,1,0:T(2,128)S(1)}, f32[1,2,2,2048]{3,2,1,0:T(2,128)}, u32[]{:S(2)}) copy-start(f32[1,2,2,2048]{3,2,1,0:T(2,128)} %copy-done.51) | copy-start | bytes 98308
  (108 other events, 473.7 us)
Sparse Core Ops, SparseCore 0:
  102.9 60.0 reduce-scatter.2
  328.2 56.7 reduce-scatter.4
where the time goes:
time: 427 us; the launch traced here: 425 us
  waiting for transfers between devices  123 us (29%)
  local copies, waits for them, and re-layouts  106 us (25%)
  matrix products  54.1 us (13%)
  blocking collectives  49.9 us (12%)
  starting transfers between devices  36.1 us (8%)
  other arithmetic  23.2 us (5%)
  between operations  16.5 us (4%)
  loops' own time  16.2 us (4%)
    reduce_scatter x2, waiting for transfers between devices, share_pattern(): lax.psum_scatter(pattern_term(radiated_cols, dirs, sub_pos, elem_pos, sha...  116 us
    unnamed x368, local copies, waits for them, and re-layouts  59 us
    psum x1, blocking collectives, local(): numerator, denominator = lax.psum((part_num, part_den), ('row', 'col'))  29.6 us
    ppermute x8, starting transfers between devices, with_halo(): lax.ppermute(tail, axis, [(i, (i + 1) % count) for i in range(ends)])  25.5 us
    all_gather x1, blocking collectives, local(): lax.all_gather(residual.astype(jnp.bfloat16), ('row', 'col'), axis=0, til...  20.3 us
    dot_general x15, matrix products, coupling(): jnp.einsum(spec, block_im, source_stack[1], preferred_element_type=jnp.fl...  19.4 us
    dot_general x15, matrix products, coupling(): jnp.einsum(spec, block_re, source_stack[0], preferred_element_type=jnp.fl...  18.3 us
    another operation x2, loops' own time, pattern_term(): stacked = lax.map(lambda begin_row: one_block(begin_row, dir_block), starts)  16 us
  transfers between devices with their start and end apart: 18, of which 7 were waited for; matrix products, arithmetic and copies ran while one was open for 5% of the time, Pallas kernels for 0%

commit v1 on v0

--- a/solution.py
+++ b/solution.py
@@ -1,8 +1,11 @@
+import functools
 import math
 
 import jax
 import jax.numpy as jnp
 from jax import lax
+from jax.experimental import pallas as pl
+from jax.experimental.pallas import tpu as pltpu
 from jax.sharding import PartitionSpec as P
 
 pi_value = 3.141592653589793
@@ -146,7 +149,7 @@
     return (products[:beams] + products[beams:], squares[:beams] + squares[beams:])
 
 
-def local(currents, library, block_ids, dirs, beam_dir):
+def by_elements(currents, library, block_ids, dirs, beam_dir):
     beams = beam_dir.shape[0]
     rows_here = currents.shape[1]
     cols_here = currents.shape[2]
@@ -241,6 +244,358 @@
     return (currents, share)
 
 
+lanes = 128
+chunk = 256
+sin_fit = (3.141592580044754, -5.167706878916943, 2.5500313770294833, -0.5980451722529145, 0.07722012475690251)
+cos_fit = (0.9999999535196061, -4.934792861473954, 4.058411954029988, -1.3318803713197287, 0.21969716737372766)
+
+
+def iota(shape, dim):
+    return lax.broadcasted_iota(jnp.int32, shape, dim)
+
+
+def turn(angle):
+    whole = jnp.round(angle)
+    rest = angle - whole
+    half = 0.5 * whole
+    sign = 1.0 - 4.0 * (half - jnp.floor(half))
+    square = rest * rest
+    sine = sin_fit[4]
+    cosine = cos_fit[4]
+    for k in (3, 2, 1, 0):
+        sine = sine * square + sin_fit[k]
+        cosine = cosine * square + cos_fit[k]
+    return cosine * sign, sine * rest * sign
+
+
+def shuffle(elems, places):
+    size = 2 * elems * places
+    row = iota((size, 1), 0)
+    kept = 2 * places
+    groups = size // lanes
+    k = row // lanes
+    q = (row % lanes) // kept
+    half = (row % kept) // places
+    p = row % places
+    goal = p * (2 * elems) + half * elems + q * groups + k
+    return (goal == iota((size, size), 1)).astype(jnp.float32).astype(jnp.bfloat16)
+
+
+def split_kernel(ranks, beams, elems, currents, ids, out):
+    _, rows, cols, packed = currents.shape
+    places = rows * cols
+    groups = lanes // beams
+    field = jnp.concatenate([currents[a, b] for a in range(2) for b in range(rows)], axis=0)
+    tiles = jnp.concatenate(
+        [field[:, i * lanes : (i + 1) * lanes] for i in range(packed // lanes)], axis=0
+    ).T
+    high = tiles.astype(jnp.bfloat16)
+    low = (tiles - high.astype(jnp.float32)).astype(jnp.bfloat16)
+    stacked = jnp.concatenate(
+        [
+            jnp.concatenate([part[k * beams : (k + 1) * beams] for k in range(groups)], axis=1)
+            for part in (high, low)
+        ],
+        axis=0,
+    )
+    moved = jnp.dot(stacked, shuffle(elems, places), preferred_element_type=jnp.float32)
+    moved = moved[:beams] + moved[beams:]
+    for bl in range(beams // ranks):
+        for p in range(places):
+            out[pl.ds(bl * places + p, ranks, stride=16), :] = moved[
+                bl * ranks : (bl + 1) * ranks, p * lanes : (p + 1) * lanes
+            ]
+    slots = ids.shape[2]
+    table = jnp.concatenate([ids[a] for a in range(rows)], axis=0).astype(jnp.float32)
+    table = jnp.concatenate([table, jnp.zeros((places, lanes - slots), jnp.float32)], axis=1)
+    table = jnp.concatenate([table, jnp.zeros_like(table)], axis=0)
+    for m in range(ranks):
+        out[m * 16 + 8 : m * 16 + 16, :] = table
+
+
+def join_kernel(ranks, beams, elems, currents, moved_in, new_currents, far, work):
+    _, rows, cols, packed = currents.shape
+    places = rows * cols
+    groups = lanes // beams
+    share = beams // ranks
+    work[...] = moved_in[...].astype(jnp.float32)
+
+    def rows_of(first):
+        return work[pl.ds(first, ranks, stride=16), :]
+
+    stacked = jnp.concatenate(
+        [
+            jnp.concatenate([rows_of(bl * places + p) for p in range(places)], axis=1)
+            for bl in range(share)
+        ],
+        axis=0,
+    ).astype(jnp.bfloat16)
+    back = lax.dot_general(
+        stacked,
+        shuffle(elems, places),
+        (((1,), (1,)), ((), ())),
+        preferred_element_type=jnp.float32,
+    )
+    tiles = jnp.concatenate([back[:, k * lanes : (k + 1) * lanes] for k in range(groups)], axis=0).T
+    kept = 2 * places
+    moved = jnp.concatenate(
+        [tiles[i * kept : (i + 1) * kept] for i in range(packed // lanes)], axis=1
+    )
+    for a in range(2):
+        for b in range(rows):
+            first = (a * rows + b) * cols
+            new_currents[a, b] = currents[a, b] - moved[first : first + cols]
+    pattern = jnp.concatenate(
+        [rows_of(8 + i) + rows_of(8 + 2 * share + i) for i in range(2 * share)], axis=0
+    )
+    far[...] = pattern.T
+
+
+def beam_kernel(
+    counts, beams, amplitude, scale, given, library, dirs, beam_dir, out,
+    blocks_wide, blocks_tall, off, sub_re, sub_im, chosen, gathered, phased, pattern, image, work,
+):
+    row_count, col_count = counts
+    ranks = row_count * col_count
+    values, elems, _ = library.shape
+    side = math.isqrt(elems)
+    share = beams // ranks
+    subs = chosen.shape[1]
+    places = subs // ranks
+    place_cols = 2
+    place_rows = places // place_cols
+    total = dirs.shape[1]
+    chunks = total // chunk
+    field_rows = share * subs
+    me = lax.axis_index("row") * col_count + lax.axis_index("col")
+    real_lane = iota((1, lanes), 1) < elems
+
+    for v in range(values):
+        block = library[v].astype(jnp.float32)
+        upper = jnp.where(real_lane, block, -block).astype(jnp.bfloat16)
+        lower = jnp.concatenate([block[:, elems:], block[:, :elems]], axis=1).astype(jnp.bfloat16)
+        both = jnp.concatenate([upper, lower], axis=0)
+        blocks_tall[v * lanes : (v + 1) * lanes, :] = both
+        blocks_wide[:, v * lanes : (v + 1) * lanes] = both
+
+    s = iota((subs, 1), 0)
+    place, rank = s // ranks, s % ranks
+    sub_row = (rank // col_count) * place_rows + place // place_cols
+    sub_col = (rank % col_count) * place_cols + place % place_cols
+    x_sub = (sub_col * side).astype(jnp.float32) - (col_count * place_cols * side - 1) / 2.0
+    y_sub = (sub_row * side).astype(jnp.float32) - (row_count * place_rows * side - 1) / 2.0
+    e = iota((elems, 1), 0)
+    x_off = (e % side).astype(jnp.float32)
+    y_off = (e // side).astype(jnp.float32)
+    for i in range(chunks):
+        cut = slice(i * chunk, (i + 1) * chunk)
+        u, v = dirs[0:1, cut], dirs[1:2, cut]
+        cosine, sine = turn(u * x_sub + v * y_sub)
+        sub_re[:, cut] = cosine
+        sub_im[:, cut] = -sine
+        cosine, sine = turn(u * x_off + v * y_off)
+        both = jnp.concatenate([cosine, -sine], axis=0)
+        high = both.astype(jnp.bfloat16)
+        off[0:lanes, cut] = high
+        off[lanes : 2 * lanes, cut] = (both - high.astype(jnp.float32)).astype(jnp.bfloat16)
+
+    def received(first):
+        return given[pl.ds(first, ranks, stride=16), :]
+
+    field = jnp.concatenate([received(i) for i in range(share * places)], axis=0)
+    ids = jnp.concatenate([received(8 + p) for p in range(places)], axis=0).astype(jnp.int32)
+
+    code = sub_row * 64 + sub_col
+    t = iota((1, subs), 1)
+    t_place, t_rank = t // ranks, t % ranks
+    t_row = (t_rank // col_count) * place_rows + t_place // place_cols
+    t_col = (t_rank % col_count) * place_cols + t_place % place_cols
+    gap = t_row * 64 + t_col - code
+    pair = jnp.full((subs, subs), -1, jnp.int32)
+    for row_off in range(5):
+        for col_off in range(5):
+            slot = 5 * row_off + col_off
+            pair = jnp.where(
+                gap == (row_off - 2) * 64 + (col_off - 2), ids[:, slot : slot + 1], pair
+            )
+    pair_adjoint = pair.astype(jnp.float32).T.astype(jnp.int32)
+
+    def choose(table):
+        for v in range(values):
+            chosen[v * subs : (v + 1) * subs, :] = (
+                (table == v).astype(jnp.float32).astype(jnp.bfloat16)
+            )
+
+    def gather(x):
+        xb = x.astype(jnp.bfloat16)
+        beside = jnp.concatenate([xb[i * subs : (i + 1) * subs] for i in range(share)], axis=1)
+        sums = jnp.dot(chosen[...], beside, preferred_element_type=jnp.float32)
+        sums = sums.astype(jnp.bfloat16)
+        for v in range(values):
+            for i in range(share):
+                gathered[i * subs : (i + 1) * subs, v * lanes : (v + 1) * lanes] = sums[
+                    v * subs : (v + 1) * subs, i * lanes : (i + 1) * lanes
+                ]
+
+    def couple(x):
+        choose(pair)
+        gather(x)
+        return lax.dot_general(
+            gathered[...],
+            blocks_wide[...],
+            (((1,), (1,)), ((), ())),
+            preferred_element_type=jnp.float32,
+        )
+
+    def couple_adj(x):
+        choose(pair_adjoint)
+        gather(x)
+        return jnp.dot(gathered[...], blocks_tall[...], preferred_element_type=jnp.float32)
+
+    def swap(x):
+        return jnp.concatenate([x[:, elems:], x[:, :elems]], axis=1)
+
+    def project(x, result):
+        total_field = x + couple(x)
+        real = jnp.where(real_lane, total_field, -total_field)
+        both = jnp.concatenate([real, swap(total_field)], axis=0).astype(jnp.bfloat16)
+        both = jnp.concatenate([both, both], axis=1)
+        for i in range(chunks):
+            cut = slice(i * chunk, (i + 1) * chunk)
+            part = jnp.dot(both, off[:, cut], preferred_element_type=jnp.float32)
+            s_re, s_im = sub_re[:, cut], sub_im[:, cut]
+            for bl in range(share):
+                p_re = part[bl * subs : (bl + 1) * subs]
+                p_im = part[field_rows + bl * subs : field_rows + (bl + 1) * subs]
+                result[bl : bl + 1, cut] = scale * jnp.sum(
+                    s_re * p_re - s_im * p_im, axis=0, keepdims=True
+                )
+                result[share + bl : share + bl + 1, cut] = scale * jnp.sum(
+                    s_re * p_im + s_im * p_re, axis=0, keepdims=True
+                )
+
+    project(field, pattern)
+
+    d = iota((1, total), 1)
+    target = jnp.concatenate(
+        [jnp.where(d == beam_dir[bl * ranks + me], amplitude, 0.0) for bl in range(share)], axis=0
+    )
+    residual = pattern[...] - jnp.concatenate([target, jnp.zeros_like(target)], axis=0)
+    rounded = residual.astype(jnp.bfloat16).astype(jnp.float32)
+    for i in range(chunks):
+        cut = slice(i * chunk, (i + 1) * chunk)
+        s_re, s_im = sub_re[:, cut], sub_im[:, cut]
+        for bl in range(share):
+            r_re = rounded[bl : bl + 1, cut]
+            r_im = rounded[share + bl : share + bl + 1, cut]
+            phased[bl * subs : (bl + 1) * subs, cut] = (s_re * r_re + s_im * r_im).astype(
+                jnp.bfloat16
+            )
+            phased[field_rows + bl * subs : field_rows + (bl + 1) * subs, cut] = (
+                s_re * r_im - s_im * r_re
+            ).astype(jnp.bfloat16)
+    sums = lax.dot_general(
+        phased[...], off[...], (((1,), (1,)), ((), ())), preferred_element_type=jnp.float32
+    )
+    sums = sums[:, :lanes] + sums[:, lanes:]
+    upper, lower = sums[:field_rows], sums[field_rows:]
+    back = scale * (jnp.where(real_lane, upper, -upper) + swap(lower))
+    gradient = back + couple_adj(back)
+    project(gradient, image)
+
+    products = jnp.sum(image[...] * residual, axis=1, keepdims=True)
+    squares = jnp.sum(image[...] * image[...], axis=1, keepdims=True)
+    step = (products[:share] + products[share:]) / (squares[:share] + squares[share:] + 1e-06)
+    for bl in range(share):
+        for p in range(places):
+            first = bl * subs + p * ranks
+            work[pl.ds(bl * places + p, ranks, stride=16), :] = (
+                gradient[first : first + ranks] * step[bl : bl + 1]
+            )
+    final = pattern[...] - image[...] * jnp.concatenate([step, step], axis=0)
+    high = final.astype(jnp.bfloat16).astype(jnp.float32)
+    both = jnp.concatenate([high, final - high], axis=0)
+    piece = total // ranks
+    for m in range(ranks):
+        work[m * 16 + 8 : m * 16 + 16, :] = both[:, m * piece : (m + 1) * piece]
+    out[...] = work[...].astype(jnp.bfloat16)
+
+
+def by_beams(currents, library, block_ids, dirs, beam_dir):
+    beams = beam_dir.shape[0]
+    _, rows_here, cols_here, _ = currents.shape
+    values, elems, _ = library.shape
+    counts = (lax.axis_size("row"), lax.axis_size("col"))
+    ranks = counts[0] * counts[1]
+    share = beams // ranks
+    subs = ranks * rows_here * cols_here
+    all_elems = subs * elems
+    total = dirs.shape[1]
+    f32, bf16 = jnp.float32, jnp.bfloat16
+    params = pltpu.CompilerParams(vmem_limit_bytes=40 * 2**20)
+
+    def exchange(x):
+        cut = x.reshape(ranks, 16, lanes)
+        return lax.all_to_all(cut, ("row", "col"), 0, 0, tiled=False).reshape(x.shape)
+
+    sent = pl.pallas_call(
+        functools.partial(split_kernel, ranks, beams, elems),
+        out_shape=jax.ShapeDtypeStruct((16 * ranks, lanes), f32),
+        compiler_params=params,
+    )(currents, block_ids)
+    vmem = pl.BlockSpec(memory_space=pltpu.VMEM)
+    results = pl.pallas_call(
+        functools.partial(
+            beam_kernel,
+            counts,
+            beams,
+            math.sqrt(all_elems) / 16.0,
+            1.0 / math.sqrt(all_elems),
+        ),
+        in_specs=[vmem, vmem, vmem, pl.BlockSpec(memory_space=pltpu.SMEM)],
+        out_shape=jax.ShapeDtypeStruct((16 * ranks, lanes), bf16),
+        scratch_shapes=[
+            pltpu.VMEM((lanes, values * lanes), bf16),
+            pltpu.VMEM((values * lanes, lanes), bf16),
+            pltpu.VMEM((2 * lanes, total), bf16),
+            pltpu.VMEM((subs, total), f32),
+            pltpu.VMEM((subs, total), f32),
+            pltpu.VMEM((values * subs, subs), bf16),
+            pltpu.VMEM((share * subs, values * lanes), bf16),
+            pltpu.VMEM((2 * share * subs, total), bf16),
+            pltpu.VMEM((2 * share, total), f32),
+            pltpu.VMEM((2 * share, total), f32),
+            pltpu.VMEM((16 * ranks, lanes), f32),
+        ],
+        compiler_params=params,
+    )(exchange(sent), library, dirs, beam_dir)
+    return pl.pallas_call(
+        functools.partial(join_kernel, ranks, beams, elems),
+        out_shape=(
+            jax.ShapeDtypeStruct(currents.shape, f32),
+            jax.ShapeDtypeStruct((total // ranks, 2 * beams), f32),
+        ),
+        scratch_shapes=[pltpu.VMEM((16 * ranks, lanes), f32)],
+        compiler_params=params,
+    )(currents, exchange(results))
+
+
+def local(currents, library, block_ids, dirs, beam_dir):
+    beams = beam_dir.shape[0]
+    _, rows_here, cols_here, packed = currents.shape
+    elems = library.shape[1]
+    ranks = lax.axis_size(("row", "col"))
+    fits = (
+        beams == 2 * ranks
+        and (rows_here, cols_here) == (2, 2)
+        and 2 * elems == lanes
+        and 2 * packed * rows_here * cols_here == lanes * lanes
+        and dirs.shape[1] == ranks * lanes
+    )
+    plan = by_beams if fits else by_elements
+    return plan(currents, library, block_ids, dirs, beam_dir)
+
+
 def solution(mesh):
     return jax.shard_map(
         local,

time: 427 us -> 38.3 us (0.09)
  waiting for transfers between devices: 123 us -> 0 us
  local copies, waits for them, and re-layouts: 106 us -> 3.92 us
  matrix products: 54.1 us -> 0 us
  starting transfers between devices: 36.1 us -> 0 us
  blocking collectives: 49.9 us -> 24.7 us
  other arithmetic: 23.2 us -> 0 us
  loops' own time: 16.2 us -> 0 us
  between operations: 16.5 us -> 0.67 us
  Pallas kernels: 0 us -> 8.58 us
    reduce_scatter x2 -> x0, waiting for transfers between devices: 116 us -> none  [share_pattern(): lax.psum_scatter(pattern_term(radiated_cols, dirs, sub_pos, elem_pos, sha...]
    unnamed x368 -> x12, local copies, waits for them, and re-layouts: 59 us -> 3.22 us
    dot_general x84 -> x0, matrix products: 54.1 us -> none  [the longest x15 19.4 us: coupling(): jnp.einsum(spec, block_im, source_stack[1], preferred_element_type=jnp.fl...]
    ppermute x16 -> x0, starting transfers between devices: 36 us -> none  [the longest x8 25.5 us: with_halo(): lax.ppermute(tail, axis, [(i, (i + 1) % count) for i in range(ends)])]
    psum x1 -> x0, blocking collectives: 29.6 us -> none  [local(): numerator, denominator = lax.psum((part_num, part_den), ('row', 'col'))]
    all_to_all x0 -> x2, blocking collectives: none -> 24.7 us  [exchange(): lax.all_to_all(cut, ('row', 'col'), 0, 0, tiled=False).reshape(x.shape)]
    all_gather x1 -> x0, blocking collectives: 20.3 us -> none  [local(): lax.all_gather(residual.astype(jnp.bfloat16), ('row', 'col'), axis=0, til...]
    another operation x3 -> x0, loops' own time: 16.2 us -> none  [the longest x2 16 us: pattern_term(): stacked = lax.map(lambda begin_row: one_block(begin_row, dir_block), starts)]
  transfers between devices with their start and end apart: 18 -> 0, of which waited for: 7 -> 0; matrix products, arithmetic and copies ran while one was open for 5% -> 0% of each run, Pallas kernels for 0% -> 0%
where the time goes in v1:
time: 38.3 us; the launch traced here: 37.9 us
  blocking collectives  24.7 us (64%)
  Pallas kernels  8.58 us (22%)
  local copies, waits for them, and re-layouts  3.92 us (10%)
  between operations  0.67 us (2%)
    all_to_all x2, blocking collectives, exchange(): lax.all_to_all(cut, ('row', 'col'), 0, 0, tiled=False).reshape(x.shape)  24.7 us
    pallas_call x1, Pallas kernels, by_beams(): pl.pallas_call(functools.partial(beam_kernel, counts, beams, math.sqrt(al...  7.07 us
    unnamed x12, local copies, waits for them, and re-layouts  3.22 us
    pallas_call x1, Pallas kernels, by_beams(): pl.pallas_call(functools.partial(join_kernel, ranks, beams, elems), out_s...  1.13 us

profile of v1, /device:TPU:0, one launch (start us, length us, event | category | flops | bytes accessed | tf_op | source)
XLA Modules:
  0.0 37.9 jit_solution(14185848368601392903)
XLA Ops:
  0.6 0.0 copy-start.1
  0.6 0.8 %copy-done.1 = f32[2,2,2,2048]{3,2,1,0:T(2,128)S(1)} copy-done((f32[2,2,2,2048]{3,2,1,0:T(2,128)S(1)}, f32[2,2,2,2048]{3,2,1,0:T(2,128)}, u32[]{:S(2)}) %copy-start.1) | copy-done | bytes 65560
  1.5 0.0 copy-start.4
  1.5 0.7 %copy-done.4 = s32[2,2,25]{2,1,0:T(2,128)S(1)} copy-done((s32[2,2,25]{2,1,0:T(2,128)S(1)}, s32[2,2,25]{2,1,0:T(2,128)}, u32[]{:S(2)}) %copy-start.4) | copy-done | bytes 424
  2.2 0.4 shard_map.68
  2.5 0.0 copy-start.3
  2.5 15.1 %all_to_all.10 = f32[16,16,128]{2,1,0:T(8,128)S(1)} all-to-all(f32[16,16,128]{2,1,0:T(8,128)S(1)} %bitcast.5), channel_id=1, replica_groups=mesh['groups'=2,'row'=4,'col'=4] {'row','col'}, dimensions={0} | all-to-all | bytes 262144 | tf_op jit(solution)/shard_map/all_to_all | solution.py:539
  17.6 0.0 copy-start.5
  17.6 0.0 copy-done.3
  17.6 0.7 %copy-done.5 = s32[32]{0:T(128)S(1)} copy-done((s32[32]{0:T(128)S(1)}, s32[32]{0:T(128)}, u32[]{:S(2)}) %copy-start.5) | copy-done | bytes 152
  18.3 0.0 copy-start
  18.3 1.0 %copy-done = bf16[32,64,128]{2,1,0:T(8,128)(2,1)S(1)} copy-done((bf16[32,64,128]{2,1,0:T(8,128)(2,1)S(1)}, bf16[32,64,128]{2,1,0:T(8,128)(2,1)}, u32[]{:S(2)}) %copy-start) | copy-done | bytes 524312
  19.3 7.1 %shard_map.69 = bf16[256,128]{1,0:T(8,128)(2,1)S(1)} custom-call(f32[256,128]{1,0:T(8,128)S(1)} %bitcast.4, bf16[32,64,128]{2,1,0:T(8,128)(2,1)S(1)} %copy-done, f32[2,2048]{1,0:T(2,128)S(1)} %copy-done.3, s32[32]{0:T(128)S(1)} %copy-done.5), custom_call_target="tpu_custom_call" | custom-call | tf_op jit(solution)/shard_map/pallas_call | solution.py:547
  26.4 0.0 copy-start.2
  26.4 9.6 %all_to_all.11 = bf16[16,16,128]{2,1,0:T(8,128)(2,1)S(1)} all-to-all(bf16[16,16,128]{2,1,0:T(8,128)(2,1)S(1)} %bitcast.6), channel_id=1, replica_groups=mesh['groups'=2,'row'=4,'col'=4] {'row','col'}, dimensions={0} | all-to-all | bytes 131072 | tf_op jit(solution)/shard_map/all_to_all | solution.py:539
  36.0 0.0 copy-done.2
  36.0 1.1 %shard_map.70 = (f32[2,2,2,2048]{3,2,1,0:T(2,128)}, f32[128,64]{1,0:T(8,128)S(1)}) custom-call(f32[2,2,2,2048]{3,2,1,0:T(2,128)S(1)} %copy-done.2, bf16[256,128]{1,0:T(8,128)(2,1)S(1)} %bitcast.7), custom_call_target="tpu_custom_call" | custom-call | tf_op jit(solution)/shard_map/pallas_call | solution.py:572
  37.2 0.7 %copy.7 = f32[128,64]{0,1:T(8,128)} copy(f32[128,64]{1,0:T(8,128)S(1)} %get-tuple-element.3) | data formatting | bytes 65536 | tf_op jit(solution)/shard_map/pallas_call | solution.py:572
Async XLA Ops:
  0.6 0.8 %copy-start.1 = (f32[2,2,2,2048]{3,2,1,0:T(2,128)S(1)}, f32[2,2,2,2048]{3,2,1,0:T(2,128)}, u32[]{:S(2)}) copy-start(f32[2,2,2,2048]{3,2,1,0:T(2,128)} %currents.3) | copy-start | bytes 196612
  1.5 0.7 %copy-start.4 = (s32[2,2,25]{2,1,0:T(2,128)S(1)}, s32[2,2,25]{2,1,0:T(2,128)}, u32[]{:S(2)}) copy-start(s32[2,2,25]{2,1,0:T(2,128)} %ids.1) | copy-start | bytes 1204
  2.5 15.1 %copy-start.3 = (f32[2,2048]{1,0:T(2,128)S(1)}, f32[2,2048]{1,0:T(2,128)}, u32[]{:S(2)}) copy-start(f32[2,2048]{1,0:T(2,128)} %dirs.1) | copy-start | bytes 49156
  17.6 0.7 %copy-start.5 = (s32[32]{0:T(128)S(1)}, s32[32]{0:T(128)}, u32[]{:S(2)}) copy-start(s32[32]{0:T(128)} %beam_dir.1) | copy-start | bytes 388
  18.3 1.0 %copy-start = (bf16[32,64,128]{2,1,0:T(8,128)(2,1)S(1)}, bf16[32,64,128]{2,1,0:T(8,128)(2,1)}, u32[]{:S(2)}) copy-start(bf16[32,64,128]{2,1,0:T(8,128)(2,1)} %library.1) | copy-start | bytes 1572868
  26.4 9.6 %copy-start.2 = (f32[2,2,2,2048]{3,2,1,0:T(2,128)S(1)}, f32[2,2,2,2048]{3,2,1,0:T(2,128)}, u32[]{:S(2)}) copy-start(f32[2,2,2,2048]{3,2,1,0:T(2,128)} %currents.3) | copy-start | bytes 196612

commit v2 on v1

--- a/solution.py
+++ b/solution.py
@@ -281,10 +281,19 @@
     return (goal == iota((size, size), 1)).astype(jnp.float32).astype(jnp.bfloat16)
 
 
-def split_kernel(ranks, beams, elems, currents, ids, out):
+def split_kernel(ranks, beams, elems, currents_far, ids_far, out, currents, ids, arrived):
+    copies = [
+        pltpu.make_async_copy(source, goal, arrived.at[i])
+        for i, (source, goal) in enumerate(((currents_far, currents), (ids_far, ids)))
+    ]
+    for copy in copies:
+        copy.start()
     _, rows, cols, packed = currents.shape
     places = rows * cols
     groups = lanes // beams
+    order = shuffle(elems, places)
+    for copy in copies:
+        copy.wait()
     field = jnp.concatenate([currents[a, b] for a in range(2) for b in range(rows)], axis=0)
     tiles = jnp.concatenate(
         [field[:, i * lanes : (i + 1) * lanes] for i in range(packed // lanes)], axis=0
@@ -298,7 +307,7 @@
         ],
         axis=0,
     )
-    moved = jnp.dot(stacked, shuffle(elems, places), preferred_element_type=jnp.float32)
+    moved = jnp.dot(stacked, order, preferred_element_type=jnp.float32)
     moved = moved[:beams] + moved[beams:]
     for bl in range(beams // ranks):
         for p in range(places):
@@ -348,15 +357,23 @@
     pattern = jnp.concatenate(
         [rows_of(8 + i) + rows_of(8 + 2 * share + i) for i in range(2 * share)], axis=0
     )
-    far[...] = pattern.T
+    far[...] = pattern
 
 
 def beam_kernel(
-    counts, beams, amplitude, scale, given, library, dirs, beam_dir, out,
-    blocks_wide, blocks_tall, off, sub_re, sub_im, chosen, gathered, phased, pattern, image, work,
+    counts, beams, amplitude, scale, given, library_far, dirs_far, beam_dir_far, out,
+    library, dirs, beam_dir, arrived, blocks_wide, blocks_tall, off, sub_re, sub_im, chosen, chosen_adj, gathered, phased, pattern, residual, image, work,
 ):
     row_count, col_count = counts
     ranks = row_count * col_count
+    copies = [
+        pltpu.make_async_copy(source, goal, arrived.at[i])
+        for i, (source, goal) in enumerate(
+            ((dirs_far, dirs), (library_far, library), (beam_dir_far, beam_dir))
+        )
+    ]
+    for copy in copies:
+        copy.start()
     values, elems, _ = library.shape
     side = math.isqrt(elems)
     share = beams // ranks
@@ -370,35 +387,10 @@
     me = lax.axis_index("row") * col_count + lax.axis_index("col")
     real_lane = iota((1, lanes), 1) < elems
 
-    for v in range(values):
-        block = library[v].astype(jnp.float32)
-        upper = jnp.where(real_lane, block, -block).astype(jnp.bfloat16)
-        lower = jnp.concatenate([block[:, elems:], block[:, :elems]], axis=1).astype(jnp.bfloat16)
-        both = jnp.concatenate([upper, lower], axis=0)
-        blocks_tall[v * lanes : (v + 1) * lanes, :] = both
-        blocks_wide[:, v * lanes : (v + 1) * lanes] = both
-
     s = iota((subs, 1), 0)
     place, rank = s // ranks, s % ranks
     sub_row = (rank // col_count) * place_rows + place // place_cols
     sub_col = (rank % col_count) * place_cols + place % place_cols
-    x_sub = (sub_col * side).astype(jnp.float32) - (col_count * place_cols * side - 1) / 2.0
-    y_sub = (sub_row * side).astype(jnp.float32) - (row_count * place_rows * side - 1) / 2.0
-    e = iota((elems, 1), 0)
-    x_off = (e % side).astype(jnp.float32)
-    y_off = (e // side).astype(jnp.float32)
-    for i in range(chunks):
-        cut = slice(i * chunk, (i + 1) * chunk)
-        u, v = dirs[0:1, cut], dirs[1:2, cut]
-        cosine, sine = turn(u * x_sub + v * y_sub)
-        sub_re[:, cut] = cosine
-        sub_im[:, cut] = -sine
-        cosine, sine = turn(u * x_off + v * y_off)
-        both = jnp.concatenate([cosine, -sine], axis=0)
-        high = both.astype(jnp.bfloat16)
-        off[0:lanes, cut] = high
-        off[lanes : 2 * lanes, cut] = (both - high.astype(jnp.float32)).astype(jnp.bfloat16)
-
     def received(first):
         return given[pl.ds(first, ranks, stride=16), :]
 
@@ -420,16 +412,16 @@
             )
     pair_adjoint = pair.astype(jnp.float32).T.astype(jnp.int32)
 
-    def choose(table):
+    def choose(goal, table):
         for v in range(values):
-            chosen[v * subs : (v + 1) * subs, :] = (
+            goal[v * subs : (v + 1) * subs, :] = (
                 (table == v).astype(jnp.float32).astype(jnp.bfloat16)
             )
 
-    def gather(x):
+    def gather(source, x):
         xb = x.astype(jnp.bfloat16)
         beside = jnp.concatenate([xb[i * subs : (i + 1) * subs] for i in range(share)], axis=1)
-        sums = jnp.dot(chosen[...], beside, preferred_element_type=jnp.float32)
+        sums = jnp.dot(source[...], beside, preferred_element_type=jnp.float32)
         sums = sums.astype(jnp.bfloat16)
         for v in range(values):
             for i in range(share):
@@ -437,9 +429,39 @@
                     v * subs : (v + 1) * subs, i * lanes : (i + 1) * lanes
                 ]
 
-    def couple(x):
-        choose(pair)
-        gather(x)
+    choose(chosen, pair)
+    gather(chosen, field)
+    choose(chosen_adj, pair_adjoint)
+
+    x_sub = (sub_col * side).astype(jnp.float32) - (col_count * place_cols * side - 1) / 2.0
+    y_sub = (sub_row * side).astype(jnp.float32) - (row_count * place_rows * side - 1) / 2.0
+    e = iota((elems, 1), 0)
+    x_off = (e % side).astype(jnp.float32)
+    y_off = (e // side).astype(jnp.float32)
+    copies[0].wait()
+    for i in range(chunks):
+        cut = slice(i * chunk, (i + 1) * chunk)
+        u, v = dirs[0:1, cut], dirs[1:2, cut]
+        cosine, sine = turn(u * x_sub + v * y_sub)
+        sub_re[:, cut] = cosine
+        sub_im[:, cut] = -sine
+        cosine, sine = turn(u * x_off + v * y_off)
+        both = jnp.concatenate([cosine, -sine], axis=0)
+        high = both.astype(jnp.bfloat16)
+        off[0:lanes, cut] = high
+        off[lanes : 2 * lanes, cut] = (both - high.astype(jnp.float32)).astype(jnp.bfloat16)
+
+    copies[1].wait()
+    copies[2].wait()
+    for v in range(values):
+        block = library[v].astype(jnp.float32)
+        upper = jnp.where(real_lane, block, -block).astype(jnp.bfloat16)
+        lower = jnp.concatenate([block[:, elems:], block[:, :elems]], axis=1).astype(jnp.bfloat16)
+        both = jnp.concatenate([upper, lower], axis=0)
+        blocks_tall[v * lanes : (v + 1) * lanes, :] = both
+        blocks_wide[:, v * lanes : (v + 1) * lanes] = both
+
+    def couple():
         return lax.dot_general(
             gathered[...],
             blocks_wide[...],
@@ -447,47 +469,45 @@
             preferred_element_type=jnp.float32,
         )
 
-    def couple_adj(x):
-        choose(pair_adjoint)
-        gather(x)
+    def couple_adj():
         return jnp.dot(gathered[...], blocks_tall[...], preferred_element_type=jnp.float32)
 
     def swap(x):
         return jnp.concatenate([x[:, elems:], x[:, :elems]], axis=1)
 
-    def project(x, result):
-        total_field = x + couple(x)
+    def radiate(x):
+        total_field = x + couple()
         real = jnp.where(real_lane, total_field, -total_field)
         both = jnp.concatenate([real, swap(total_field)], axis=0).astype(jnp.bfloat16)
-        both = jnp.concatenate([both, both], axis=1)
-        for i in range(chunks):
-            cut = slice(i * chunk, (i + 1) * chunk)
-            part = jnp.dot(both, off[:, cut], preferred_element_type=jnp.float32)
-            s_re, s_im = sub_re[:, cut], sub_im[:, cut]
-            for bl in range(share):
-                p_re = part[bl * subs : (bl + 1) * subs]
-                p_im = part[field_rows + bl * subs : field_rows + (bl + 1) * subs]
-                result[bl : bl + 1, cut] = scale * jnp.sum(
-                    s_re * p_re - s_im * p_im, axis=0, keepdims=True
-                )
-                result[share + bl : share + bl + 1, cut] = scale * jnp.sum(
-                    s_re * p_im + s_im * p_re, axis=0, keepdims=True
-                )
-
-    project(field, pattern)
-
-    d = iota((1, total), 1)
-    target = jnp.concatenate(
-        [jnp.where(d == beam_dir[bl * ranks + me], amplitude, 0.0) for bl in range(share)], axis=0
-    )
-    residual = pattern[...] - jnp.concatenate([target, jnp.zeros_like(target)], axis=0)
-    rounded = residual.astype(jnp.bfloat16).astype(jnp.float32)
+        return jnp.concatenate([both, both], axis=1)
+
+    def project(radiated, cut):
+        part = jnp.dot(radiated, off[:, cut], preferred_element_type=jnp.float32)
+        s_re, s_im = sub_re[:, cut], sub_im[:, cut]
+        re, im = [], []
+        for bl in range(share):
+            p_re = part[bl * subs : (bl + 1) * subs]
+            p_im = part[field_rows + bl * subs : field_rows + (bl + 1) * subs]
+            re.append(jnp.sum(s_re * p_re - s_im * p_im, axis=0, keepdims=True))
+            im.append(jnp.sum(s_re * p_im + s_im * p_re, axis=0, keepdims=True))
+        return scale * jnp.concatenate(re + im, axis=0)
+
+    radiated = radiate(field)
+    beam = iota((2 * share, 1), 0)
+    place = jnp.full((2 * share, 1), -1, jnp.int32)
+    for bl in range(share):
+        place = jnp.where(beam == bl, beam_dir[bl * ranks + me], place)
     for i in range(chunks):
         cut = slice(i * chunk, (i + 1) * chunk)
+        found = project(radiated, cut)
+        pattern[:, cut] = found
+        rest = found - jnp.where(iota((1, chunk), 1) + i * chunk == place, amplitude, 0.0)
+        residual[:, cut] = rest
+        rounded = rest.astype(jnp.bfloat16).astype(jnp.float32)
         s_re, s_im = sub_re[:, cut], sub_im[:, cut]
         for bl in range(share):
-            r_re = rounded[bl : bl + 1, cut]
-            r_im = rounded[share + bl : share + bl + 1, cut]
+            r_re = rounded[bl : bl + 1]
+            r_im = rounded[share + bl : share + bl + 1]
             phased[bl * subs : (bl + 1) * subs, cut] = (s_re * r_re + s_im * r_im).astype(
                 jnp.bfloat16
             )
@@ -500,11 +520,20 @@
     sums = sums[:, :lanes] + sums[:, lanes:]
     upper, lower = sums[:field_rows], sums[field_rows:]
     back = scale * (jnp.where(real_lane, upper, -upper) + swap(lower))
-    gradient = back + couple_adj(back)
-    project(gradient, image)
-
-    products = jnp.sum(image[...] * residual, axis=1, keepdims=True)
-    squares = jnp.sum(image[...] * image[...], axis=1, keepdims=True)
+    gather(chosen_adj, back)
+    gradient = back + couple_adj()
+    gather(chosen, gradient)
+    radiated = radiate(gradient)
+    products = jnp.zeros((2 * share, chunk), jnp.float32)
+    squares = jnp.zeros((2 * share, chunk), jnp.float32)
+    for i in range(chunks):
+        cut = slice(i * chunk, (i + 1) * chunk)
+        found = project(radiated, cut)
+        image[:, cut] = found
+        products = products + found * residual[:, cut]
+        squares = squares + found * found
+    products = jnp.sum(products, axis=1, keepdims=True)
+    squares = jnp.sum(squares, axis=1, keepdims=True)
     step = (products[:share] + products[share:]) / (squares[:share] + squares[share:] + 1e-06)
     for bl in range(share):
         for p in range(places):
@@ -534,15 +563,26 @@
     f32, bf16 = jnp.float32, jnp.bfloat16
     params = pltpu.CompilerParams(vmem_limit_bytes=40 * 2**20)
 
+    anywhere = pl.BlockSpec(memory_space=pltpu.HBM)
+
+    def keep(x):
+        return pltpu.with_memory_space_constraint(x, pltpu.HBM)
+
     def exchange(x):
         cut = x.reshape(ranks, 16, lanes)
         return lax.all_to_all(cut, ("row", "col"), 0, 0, tiled=False).reshape(x.shape)
 
     sent = pl.pallas_call(
         functools.partial(split_kernel, ranks, beams, elems),
+        in_specs=[anywhere, anywhere],
         out_shape=jax.ShapeDtypeStruct((16 * ranks, lanes), f32),
+        scratch_shapes=[
+            pltpu.VMEM(currents.shape, f32),
+            pltpu.VMEM(block_ids.shape, jnp.int32),
+            pltpu.SemaphoreType.DMA((2,)),
+        ],
         compiler_params=params,
-    )(currents, block_ids)
+    )(keep(currents), keep(block_ids))
     vmem = pl.BlockSpec(memory_space=pltpu.VMEM)
     results = pl.pallas_call(
         functools.partial(
@@ -552,32 +592,39 @@
             math.sqrt(all_elems) / 16.0,
             1.0 / math.sqrt(all_elems),
         ),
-        in_specs=[vmem, vmem, vmem, pl.BlockSpec(memory_space=pltpu.SMEM)],
+        in_specs=[vmem, anywhere, anywhere, anywhere],
         out_shape=jax.ShapeDtypeStruct((16 * ranks, lanes), bf16),
         scratch_shapes=[
+            pltpu.VMEM(library.shape, bf16),
+            pltpu.VMEM(dirs.shape, f32),
+            pltpu.SMEM(beam_dir.shape, jnp.int32),
+            pltpu.SemaphoreType.DMA((3,)),
             pltpu.VMEM((lanes, values * lanes), bf16),
             pltpu.VMEM((values * lanes, lanes), bf16),
             pltpu.VMEM((2 * lanes, total), bf16),
             pltpu.VMEM((subs, total), f32),
             pltpu.VMEM((subs, total), f32),
             pltpu.VMEM((values * subs, subs), bf16),
+            pltpu.VMEM((values * subs, subs), bf16),
             pltpu.VMEM((share * subs, values * lanes), bf16),
             pltpu.VMEM((2 * share * subs, total), bf16),
+            pltpu.VMEM((2 * share, total), f32),
             pltpu.VMEM((2 * share, total), f32),
             pltpu.VMEM((2 * share, total), f32),
             pltpu.VMEM((16 * ranks, lanes), f32),
         ],
         compiler_params=params,
-    )(exchange(sent), library, dirs, beam_dir)
-    return pl.pallas_call(
+    )(exchange(sent), keep(library), keep(dirs), keep(beam_dir))
+    new_currents, far = pl.pallas_call(
         functools.partial(join_kernel, ranks, beams, elems),
         out_shape=(
             jax.ShapeDtypeStruct(currents.shape, f32),
-            jax.ShapeDtypeStruct((total // ranks, 2 * beams), f32),
+            jax.ShapeDtypeStruct((2 * beams, total // ranks), f32),
         ),
         scratch_shapes=[pltpu.VMEM((16 * ranks, lanes), f32)],
         compiler_params=params,
     )(currents, exchange(results))
+    return new_currents, far.T
 
 
 def local(currents, library, block_ids, dirs, beam_dir):

time: 38.3 us -> 35.1 us (0.916)
  local copies, waits for them, and re-layouts: 3.92 us -> 0.01 us
  Pallas kernels: 8.58 us -> 9.49 us
    unnamed x12 -> x2, local copies, waits for them, and re-layouts: 3.22 us -> 0.01 us
    pallas_call x1, Pallas kernels: 0.38 us -> 1.14 us  [by_beams(): pl.pallas_call(functools.partial(split_kernel, ranks, beams, elems), in_s...]
    pallas_call x1 -> x0, local copies, waits for them, and re-layouts: 0.7 us -> none  [by_beams(): pl.pallas_call(functools.partial(join_kernel, ranks, beams, elems), out_s...]
where the time goes in v2:
time: 35.1 us; the launch traced here: 34.9 us
  blocking collectives  24.7 us (70%)
  Pallas kernels  9.49 us (27%)
  between operations  0.65 us (2%)
    all_to_all x2, blocking collectives, exchange(): lax.all_to_all(cut, ('row', 'col'), 0, 0, tiled=False).reshape(x.shape)  24.7 us
    pallas_call x1, Pallas kernels, by_beams(): pl.pallas_call(functools.partial(beam_kernel, counts, beams, math.sqrt(al...  7.23 us
    pallas_call x1, Pallas kernels, by_beams(): pl.pallas_call(functools.partial(split_kernel, ranks, beams, elems), in_s...  1.14 us
    pallas_call x1, Pallas kernels, by_beams(): pl.pallas_call(functools.partial(join_kernel, ranks, beams, elems), out_s...  1.12 us

profile of v2, /device:TPU:0, one launch (start us, length us, event | category | flops | bytes accessed | tf_op | source)
XLA Modules:
  0.0 34.9 jit_solution(14678322210716114548)
XLA Ops:
  0.6 1.1 %shard_map.68 = f32[256,128]{1,0:T(8,128)S(1)} custom-call(f32[2,2,2,2048]{3,2,1,0:T(2,128)} %currents.1, s32[2,2,25]{2,1,0:T(2,128)} %ids_far.1), custom_call_target="tpu_custom_call" | custom-call | tf_op jit(solution)/shard_map/pallas_call | solution.py:575
  1.8 15.1 %all_to_all.10 = f32[16,16,128]{2,1,0:T(8,128)S(1)} all-to-all(f32[16,16,128]{2,1,0:T(8,128)S(1)} %bitcast.6), channel_id=1, replica_groups=mesh['groups'=2,'row'=4,'col'=4] {'row','col'}, dimensions={0} | all-to-all | bytes 262144 | tf_op jit(solution)/shard_map/all_to_all | solution.py:573
  16.9 7.2 %shard_map.69 = bf16[256,128]{1,0:T(8,128)(2,1)S(1)} custom-call(f32[256,128]{1,0:T(8,128)S(1)} %bitcast.5, bf16[32,64,128]{2,1,0:T(8,128)(2,1)} %library_far.1, f32[2,2048]{1,0:T(2,128)} %dirs_far.1, s32[32]{0:T(128)} %beam_dir_far.1), custom_call_target="tpu_custom_call" | custom-call | tf_op jit(solution)/shard_map/pallas_call | solution.py:587
  24.1 0.0 copy-start
  24.1 9.6 %all_to_all.11 = bf16[16,16,128]{2,1,0:T(8,128)(2,1)S(1)} all-to-all(bf16[16,16,128]{2,1,0:T(8,128)(2,1)S(1)} %bitcast.7), channel_id=1, replica_groups=mesh['groups'=2,'row'=4,'col'=4] {'row','col'}, dimensions={0} | all-to-all | bytes 131072 | tf_op jit(solution)/shard_map/all_to_all | solution.py:573
  33.7 0.0 copy-done
  33.7 1.1 %shard_map.70 = (f32[2,2,2,2048]{3,2,1,0:T(2,128)}, f32[64,128]{1,0:T(8,128)}) custom-call(f32[2,2,2,2048]{3,2,1,0:T(2,128)S(1)} %copy-done, bf16[256,128]{1,0:T(8,128)(2,1)S(1)} %bitcast.8), custom_call_target="tpu_custom_call" | custom-call | tf_op jit(solution)/shard_map/pallas_call | solution.py:618
Async XLA Ops:
  24.1 9.6 %copy-start = (f32[2,2,2,2048]{3,2,1,0:T(2,128)S(1)}, f32[2,2,2,2048]{3,2,1,0:T(2,128)}, u32[]{:S(2)}) copy-start(f32[2,2,2,2048]{3,2,1,0:T(2,128)} %currents.1) | copy-start | bytes 196612

commit v3 on v2

--- a/solution.py
+++ b/solution.py
@@ -246,6 +246,7 @@
 
 lanes = 128
 chunk = 256
+message = 24
 sin_fit = (3.141592580044754, -5.167706878916943, 2.5500313770294833, -0.5980451722529145, 0.07722012475690251)
 cos_fit = (0.9999999535196061, -4.934792861473954, 4.058411954029988, -1.3318803713197287, 0.21969716737372766)
 
@@ -281,10 +282,23 @@
     return (goal == iota((size, size), 1)).astype(jnp.float32).astype(jnp.bfloat16)
 
 
-def split_kernel(ranks, beams, elems, currents_far, ids_far, out, currents, ids, arrived):
+def split_kernel(
+    counts, beams, elems, currents_far, ids_far, library_far, dirs_far, beam_dir_far,
+    out, library, dirs, aims, currents, ids, beam_dir, work, arrived,
+):
+    ranks = counts[0] * counts[1]
+    me = lax.axis_index("row") * counts[1] + lax.axis_index("col")
     copies = [
         pltpu.make_async_copy(source, goal, arrived.at[i])
-        for i, (source, goal) in enumerate(((currents_far, currents), (ids_far, ids)))
+        for i, (source, goal) in enumerate(
+            (
+                (currents_far, currents),
+                (ids_far, ids),
+                (library_far, library),
+                (dirs_far, dirs),
+                (beam_dir_far, beam_dir),
+            )
+        )
     ]
     for copy in copies:
         copy.start()
@@ -292,7 +306,7 @@
     places = rows * cols
     groups = lanes // beams
     order = shuffle(elems, places)
-    for copy in copies:
+    for copy in copies[:2]:
         copy.wait()
     field = jnp.concatenate([currents[a, b] for a in range(2) for b in range(rows)], axis=0)
     tiles = jnp.concatenate(
@@ -308,18 +322,30 @@
         axis=0,
     )
     moved = jnp.dot(stacked, order, preferred_element_type=jnp.float32)
-    moved = moved[:beams] + moved[beams:]
-    for bl in range(beams // ranks):
-        for p in range(places):
-            out[pl.ds(bl * places + p, ranks, stride=16), :] = moved[
-                bl * ranks : (bl + 1) * ranks, p * lanes : (p + 1) * lanes
-            ]
+    share = beams // ranks
+    kept = share * places
+    for half in range(2):
+        for bl in range(share):
+            first = half * beams + bl * ranks
+            for p in range(places):
+                row = half * kept + bl * places + p
+                work[pl.ds(row, ranks, stride=message), :] = moved[
+                    first : first + ranks, p * lanes : (p + 1) * lanes
+                ]
     slots = ids.shape[2]
     table = jnp.concatenate([ids[a] for a in range(rows)], axis=0).astype(jnp.float32)
     table = jnp.concatenate([table, jnp.zeros((places, lanes - slots), jnp.float32)], axis=1)
     table = jnp.concatenate([table, jnp.zeros_like(table)], axis=0)
     for m in range(ranks):
-        out[m * 16 + 8 : m * 16 + 16, :] = table
+        work[m * message + 2 * kept : (m + 1) * message, :] = table
+    out[...] = work[...].astype(jnp.bfloat16)
+    for copy in copies[2:]:
+        copy.wait()
+    row = iota(aims.shape, 0)
+    aim = jnp.full(aims.shape, -1, jnp.int32)
+    for bl in range(share):
+        aim = jnp.where(row == bl, beam_dir[bl * ranks + me], aim)
+    aims[...] = aim
 
 
 def join_kernel(ranks, beams, elems, currents, moved_in, new_currents, far, work):
@@ -361,19 +387,12 @@
 
 
 def beam_kernel(
-    counts, beams, amplitude, scale, given, library_far, dirs_far, beam_dir_far, out,
-    library, dirs, beam_dir, arrived, blocks_wide, blocks_tall, off, sub_re, sub_im, chosen, chosen_adj, gathered, phased, pattern, residual, image, work,
+    counts, beams, amplitude, scale, given, library, dirs, aims, out,
+    blocks_wide, blocks_tall, off, sub_re, sub_im, chosen, chosen_adj, gathered, phased,
+    pattern, residual, image, opened, work,
 ):
     row_count, col_count = counts
     ranks = row_count * col_count
-    copies = [
-        pltpu.make_async_copy(source, goal, arrived.at[i])
-        for i, (source, goal) in enumerate(
-            ((dirs_far, dirs), (library_far, library), (beam_dir_far, beam_dir))
-        )
-    ]
-    for copy in copies:
-        copy.start()
     values, elems, _ = library.shape
     side = math.isqrt(elems)
     share = beams // ranks
@@ -384,7 +403,6 @@
     total = dirs.shape[1]
     chunks = total // chunk
     field_rows = share * subs
-    me = lax.axis_index("row") * col_count + lax.axis_index("col")
     real_lane = iota((1, lanes), 1) < elems
 
     s = iota((subs, 1), 0)
@@ -392,10 +410,13 @@
     sub_row = (rank // col_count) * place_rows + place // place_cols
     sub_col = (rank % col_count) * place_cols + place % place_cols
     def received(first):
-        return given[pl.ds(first, ranks, stride=16), :]
-
-    field = jnp.concatenate([received(i) for i in range(share * places)], axis=0)
-    ids = jnp.concatenate([received(8 + p) for p in range(places)], axis=0).astype(jnp.int32)
+        return opened[pl.ds(first, ranks, stride=message), :]
+
+    opened[...] = given[...].astype(jnp.float32)
+    kept = share * places
+    field = jnp.concatenate([received(i) + received(kept + i) for i in range(kept)], axis=0)
+    ids = jnp.concatenate([received(2 * kept + p) for p in range(places)], axis=0)
+    ids = ids.astype(jnp.int32)
 
     code = sub_row * 64 + sub_col
     t = iota((1, subs), 1)
@@ -438,7 +459,6 @@
     e = iota((elems, 1), 0)
     x_off = (e % side).astype(jnp.float32)
     y_off = (e // side).astype(jnp.float32)
-    copies[0].wait()
     for i in range(chunks):
         cut = slice(i * chunk, (i + 1) * chunk)
         u, v = dirs[0:1, cut], dirs[1:2, cut]
@@ -451,8 +471,6 @@
         off[0:lanes, cut] = high
         off[lanes : 2 * lanes, cut] = (both - high.astype(jnp.float32)).astype(jnp.bfloat16)
 
-    copies[1].wait()
-    copies[2].wait()
     for v in range(values):
         block = library[v].astype(jnp.float32)
         upper = jnp.where(real_lane, block, -block).astype(jnp.bfloat16)
@@ -493,10 +511,7 @@
         return scale * jnp.concatenate(re + im, axis=0)
 
     radiated = radiate(field)
-    beam = iota((2 * share, 1), 0)
-    place = jnp.full((2 * share, 1), -1, jnp.int32)
-    for bl in range(share):
-        place = jnp.where(beam == bl, beam_dir[bl * ranks + me], place)
+    place = aims[0 : 2 * share, 0:1]
     for i in range(chunks):
         cut = slice(i * chunk, (i + 1) * chunk)
         found = project(radiated, cut)
@@ -563,27 +578,31 @@
     f32, bf16 = jnp.float32, jnp.bfloat16
     params = pltpu.CompilerParams(vmem_limit_bytes=40 * 2**20)
 
-    anywhere = pl.BlockSpec(memory_space=pltpu.HBM)
-
     def keep(x):
         return pltpu.with_memory_space_constraint(x, pltpu.HBM)
 
     def exchange(x):
-        cut = x.reshape(ranks, 16, lanes)
+        cut = x.reshape(ranks, -1, lanes)
         return lax.all_to_all(cut, ("row", "col"), 0, 0, tiled=False).reshape(x.shape)
 
-    sent = pl.pallas_call(
-        functools.partial(split_kernel, ranks, beams, elems),
-        in_specs=[anywhere, anywhere],
-        out_shape=jax.ShapeDtypeStruct((16 * ranks, lanes), f32),
+    sent, library_near, dirs_near, aims = pl.pallas_call(
+        functools.partial(split_kernel, counts, beams, elems),
+        in_specs=[pl.BlockSpec(memory_space=pltpu.HBM)] * 5,
+        out_shape=(
+            jax.ShapeDtypeStruct((message * ranks, lanes), bf16),
+            jax.ShapeDtypeStruct(library.shape, bf16),
+            jax.ShapeDtypeStruct(dirs.shape, f32),
+            jax.ShapeDtypeStruct((8, lanes), jnp.int32),
+        ),
         scratch_shapes=[
             pltpu.VMEM(currents.shape, f32),
             pltpu.VMEM(block_ids.shape, jnp.int32),
-            pltpu.SemaphoreType.DMA((2,)),
+            pltpu.SMEM(beam_dir.shape, jnp.int32),
+            pltpu.VMEM((message * ranks, lanes), f32),
+            pltpu.SemaphoreType.DMA((5,)),
         ],
         compiler_params=params,
-    )(keep(currents), keep(block_ids))
-    vmem = pl.BlockSpec(memory_space=pltpu.VMEM)
+    )(keep(currents), keep(block_ids), keep(library), keep(dirs), keep(beam_dir))
     results = pl.pallas_call(
         functools.partial(
             beam_kernel,
@@ -592,13 +611,8 @@
             math.sqrt(all_elems) / 16.0,
             1.0 / math.sqrt(all_elems),
         ),
-        in_specs=[vmem, anywhere, anywhere, anywhere],
         out_shape=jax.ShapeDtypeStruct((16 * ranks, lanes), bf16),
         scratch_shapes=[
-            pltpu.VMEM(library.shape, bf16),
-            pltpu.VMEM(dirs.shape, f32),
-            pltpu.SMEM(beam_dir.shape, jnp.int32),
-            pltpu.SemaphoreType.DMA((3,)),
             pltpu.VMEM((lanes, values * lanes), bf16),
             pltpu.VMEM((values * lanes, lanes), bf16),
             pltpu.VMEM((2 * lanes, total), bf16),
@@ -611,10 +625,11 @@
             pltpu.VMEM((2 * share, total), f32),
             pltpu.VMEM((2 * share, total), f32),
             pltpu.VMEM((2 * share, total), f32),
+            pltpu.VMEM((message * ranks, lanes), f32),
             pltpu.VMEM((16 * ranks, lanes), f32),
         ],
         compiler_params=params,
-    )(exchange(sent), keep(library), keep(dirs), keep(beam_dir))
+    )(exchange(sent), library_near, dirs_near, aims)
     new_currents, far = pl.pallas_call(
         functools.partial(join_kernel, ranks, beams, elems),
         out_shape=(

time: 35.1 us -> 33.7 us (0.960)
  Pallas kernels: 9.49 us -> 8.59 us
  blocking collectives: 24.7 us -> 24.2 us
    pallas_call x1, Pallas kernels: 7.23 us -> 6.29 us  [by_beams(): pl.pallas_call(functools.partial(beam_kernel, counts, beams, math.sqrt(al...]
    all_to_all x2, blocking collectives: 24.7 us -> 24.2 us  [exchange(): lax.all_to_all(cut, ('row', 'col'), 0, 0, tiled=False).reshape(x.shape)]
where the time goes in v3:
time: 33.7 us; the launch traced here: 33.4 us
  blocking collectives  24.2 us (72%)
  Pallas kernels  8.59 us (25%)
  between operations  0.65 us (2%)
    all_to_all x2, blocking collectives, exchange(): lax.all_to_all(cut, ('row', 'col'), 0, 0, tiled=False).reshape(x.shape)  24.2 us
    pallas_call x1, Pallas kernels, by_beams(): pl.pallas_call(functools.partial(beam_kernel, counts, beams, math.sqrt(al...  6.29 us
    pallas_call x1, Pallas kernels, by_beams(): pl.pallas_call(functools.partial(split_kernel, counts, beams, elems), in_...  1.18 us
    pallas_call x1, Pallas kernels, by_beams(): pl.pallas_call(functools.partial(join_kernel, ranks, beams, elems), out_s...  1.12 us

profile of v3, /device:TPU:0, one launch (start us, length us, event | category | flops | bytes accessed | tf_op | source)
XLA Modules:
  0.0 33.4 jit_solution(5599615075523662869)
XLA Ops:
  0.6 1.2 %shard_map.68 = (bf16[384,128]{1,0:T(8,128)(2,1)S(1)}, bf16[32,64,128]{2,1,0:T(8,128)(2,1)S(1)}, f32[2,2048]{1,0:T(2,128)S(1)}, s32[8,128]{1,0:T(8,128)S(1)}) custom-call(f32[2,2,2,2048]{3,2,1,0:T(2,128)} %currents.1, s32[2,2,25]{2,1,0:T(2,128)} %ids_far.1, bf16[32,64,128]{2,1,0:T(8,128)(2,1)} %library_far.1, f32[2,2048]{1,0:T(2,128)} %dirs_far.1, ...), custom_call_target="tpu_custom_call" | custom-call | tf_op jit(solution)/shard_map/pallas_call | solution.py:588
  1.8 14.6 %all_to_all.10 = bf16[16,24,128]{2,1,0:T(8,128)(2,1)S(1)} all-to-all(bf16[16,24,128]{2,1,0:T(8,128)(2,1)S(1)} %bitcast.8), channel_id=1, replica_groups=mesh['groups'=2,'row'=4,'col'=4] {'row','col'}, dimensions={0} | all-to-all | bytes 196608 | tf_op jit(solution)/shard_map/all_to_all | solution.py:586
  16.4 6.3 %shard_map.69 = bf16[256,128]{1,0:T(8,128)(2,1)S(1)} custom-call(bf16[384,128]{1,0:T(8,128)(2,1)S(1)} %bitcast.5, bf16[32,64,128]{2,1,0:T(8,128)(2,1)S(1)} %get-tuple-element.9.library, f32[2,2048]{1,0:T(2,128)S(1)} %get-tuple-element.10.dirs, s32[8,128]{1,0:T(8,128)S(1)} %get-tuple-element.11.aims), custom_call_target="tpu_custom_call" | custom-call | tf_op jit(solution)/shard_map/pallas_call | solution.py:606
  22.7 0.0 copy-start
  22.7 9.6 %all_to_all.11 = bf16[16,16,128]{2,1,0:T(8,128)(2,1)S(1)} all-to-all(bf16[16,16,128]{2,1,0:T(8,128)(2,1)S(1)} %bitcast.7), channel_id=1, replica_groups=mesh['groups'=2,'row'=4,'col'=4] {'row','col'}, dimensions={0} | all-to-all | bytes 131072 | tf_op jit(solution)/shard_map/all_to_all | solution.py:586
  32.3 0.0 copy-done
  32.3 1.1 %shard_map.70 = (f32[2,2,2,2048]{3,2,1,0:T(2,128)}, f32[64,128]{1,0:T(8,128)}) custom-call(f32[2,2,2,2048]{3,2,1,0:T(2,128)S(1)} %copy-done, bf16[256,128]{1,0:T(8,128)(2,1)S(1)} %bitcast.6), custom_call_target="tpu_custom_call" | custom-call | tf_op jit(solution)/shard_map/pallas_call | solution.py:633
Async XLA Ops:
  22.7 9.6 %copy-start = (f32[2,2,2,2048]{3,2,1,0:T(2,128)S(1)}, f32[2,2,2,2048]{3,2,1,0:T(2,128)}, u32[]{:S(2)}) copy-start(f32[2,2,2,2048]{3,2,1,0:T(2,128)} %currents.1) | copy-start | bytes 196612

commit v4 on v3

--- a/solution.py
+++ b/solution.py
@@ -396,7 +396,7 @@
     values, elems, _ = library.shape
     side = math.isqrt(elems)
     share = beams // ranks
-    subs = chosen.shape[1]
+    subs = chosen.shape[0]
     places = subs // ranks
     place_cols = 2
     place_rows = places // place_cols
@@ -434,38 +434,60 @@
     pair_adjoint = pair.astype(jnp.float32).T.astype(jnp.int32)
 
     def choose(goal, table):
-        for v in range(values):
-            goal[v * subs : (v + 1) * subs, :] = (
-                (table == v).astype(jnp.float32).astype(jnp.bfloat16)
+        twice = jnp.concatenate([table, table], axis=1)
+        value = iota((1, 2 * subs), 1) // subs
+        for v in range(0, values, 2):
+            goal[:, v * subs : (v + 2) * subs] = (
+                (twice == value + v).astype(jnp.float32).astype(jnp.bfloat16)
             )
 
-    def gather(source, x):
-        xb = x.astype(jnp.bfloat16)
-        beside = jnp.concatenate([xb[i * subs : (i + 1) * subs] for i in range(share)], axis=1)
-        sums = jnp.dot(source[...], beside, preferred_element_type=jnp.float32)
-        sums = sums.astype(jnp.bfloat16)
-        for v in range(values):
-            for i in range(share):
-                gathered[i * subs : (i + 1) * subs, v * lanes : (v + 1) * lanes] = sums[
-                    v * subs : (v + 1) * subs, i * lanes : (i + 1) * lanes
-                ]
-
     choose(chosen, pair)
-    gather(chosen, field)
     choose(chosen_adj, pair_adjoint)
 
-    x_sub = (sub_col * side).astype(jnp.float32) - (col_count * place_cols * side - 1) / 2.0
-    y_sub = (sub_row * side).astype(jnp.float32) - (row_count * place_rows * side - 1) / 2.0
-    e = iota((elems, 1), 0)
-    x_off = (e % side).astype(jnp.float32)
-    y_off = (e // side).astype(jnp.float32)
+    def multiply(x, y):
+        return x[0] * y[0] - x[1] * y[1], x[0] * y[1] + x[1] * y[0]
+
+    half_x = (col_count * place_cols * side - 1) / 2.0
+    half_y = (row_count * place_rows * side - 1) / 2.0
+
+    def sub_turns(along, count, kept, half):
+        r = iota((count * kept, 1), 0)
+        position = ((r % count) * kept + r // count) * side
+        return turn(along * (position.astype(jnp.float32) - half))
+
     for i in range(chunks):
         cut = slice(i * chunk, (i + 1) * chunk)
         u, v = dirs[0:1, cut], dirs[1:2, cut]
-        cosine, sine = turn(u * x_sub + v * y_sub)
-        sub_re[:, cut] = cosine
-        sub_im[:, cut] = -sine
-        cosine, sine = turn(u * x_off + v * y_off)
+        x_turn = sub_turns(u, col_count, place_cols, half_x)
+        y_turn = sub_turns(v, row_count, place_rows, half_y)
+        for p in range(places):
+            x0 = (p % place_cols) * col_count
+            y0 = (p // place_cols) * row_count
+            xs = [jnp.concatenate([t[x0 : x0 + col_count]] * row_count, axis=0) for t in x_turn]
+            ys = [
+                jnp.concatenate(
+                    [
+                        jnp.broadcast_to(t[y0 + k : y0 + k + 1], (col_count, chunk))
+                        for k in range(row_count)
+                    ],
+                    axis=0,
+                )
+                for t in y_turn
+            ]
+            cosine, sine = multiply(xs, ys)
+            sub_re[p * ranks : (p + 1) * ranks, cut] = cosine
+            sub_im[p * ranks : (p + 1) * ranks, cut] = -sine
+        steps = iota((side, 1), 0).astype(jnp.float32)
+        x_turn, y_turn = turn(u * steps), turn(v * steps)
+        cosine, sine = multiply(
+            [jnp.concatenate([t] * side, axis=0) for t in x_turn],
+            [
+                jnp.concatenate(
+                    [jnp.broadcast_to(t[k : k + 1], (side, chunk)) for k in range(side)], axis=0
+                )
+                for t in y_turn
+            ],
+        )
         both = jnp.concatenate([cosine, -sine], axis=0)
         high = both.astype(jnp.bfloat16)
         off[0:lanes, cut] = high
@@ -479,22 +501,38 @@
         blocks_tall[v * lanes : (v + 1) * lanes, :] = both
         blocks_wide[:, v * lanes : (v + 1) * lanes] = both
 
-    def couple():
-        return lax.dot_general(
-            gathered[...],
-            blocks_wide[...],
-            (((1,), (1,)), ((), ())),
-            preferred_element_type=jnp.float32,
+    def spread(every):
+        every = every.astype(jnp.bfloat16)
+        for v in range(values):
+            for i in range(share):
+                gathered[v * subs : (v + 1) * subs, i * lanes : (i + 1) * lanes] = every[
+                    i * subs : (i + 1) * subs, v * lanes : (v + 1) * lanes
+                ]
+
+    def collect(source):
+        sums = jnp.dot(source[...], gathered[...], preferred_element_type=jnp.float32)
+        return jnp.concatenate([sums[:, i * lanes : (i + 1) * lanes] for i in range(share)], axis=0)
+
+    def couple(x):
+        spread(
+            lax.dot_general(
+                x.astype(jnp.bfloat16),
+                blocks_tall[...],
+                (((1,), (1,)), ((), ())),
+                preferred_element_type=jnp.float32,
+            )
         )
-
-    def couple_adj():
-        return jnp.dot(gathered[...], blocks_tall[...], preferred_element_type=jnp.float32)
+        return collect(chosen)
+
+    def couple_adj(x):
+        spread(jnp.dot(x.astype(jnp.bfloat16), blocks_wide[...], preferred_element_type=jnp.float32))
+        return collect(chosen_adj)
 
     def swap(x):
         return jnp.concatenate([x[:, elems:], x[:, :elems]], axis=1)
 
     def radiate(x):
-        total_field = x + couple()
+        total_field = x + couple(x)
         real = jnp.where(real_lane, total_field, -total_field)
         both = jnp.concatenate([real, swap(total_field)], axis=0).astype(jnp.bfloat16)
         return jnp.concatenate([both, both], axis=1)
@@ -535,9 +573,7 @@
     sums = sums[:, :lanes] + sums[:, lanes:]
     upper, lower = sums[:field_rows], sums[field_rows:]
     back = scale * (jnp.where(real_lane, upper, -upper) + swap(lower))
-    gather(chosen_adj, back)
-    gradient = back + couple_adj()
-    gather(chosen, gradient)
+    gradient = back + couple_adj(back)
     radiated = radiate(gradient)
     products = jnp.zeros((2 * share, chunk), jnp.float32)
     squares = jnp.zeros((2 * share, chunk), jnp.float32)
@@ -618,9 +654,9 @@
             pltpu.VMEM((2 * lanes, total), bf16),
             pltpu.VMEM((subs, total), f32),
             pltpu.VMEM((subs, total), f32),
-            pltpu.VMEM((values * subs, subs), bf16),
-            pltpu.VMEM((values * subs, subs), bf16),
-            pltpu.VMEM((share * subs, values * lanes), bf16),
+            pltpu.VMEM((subs, values * subs), bf16),
+            pltpu.VMEM((subs, values * subs), bf16),
+            pltpu.VMEM((values * subs, share * lanes), bf16),
             pltpu.VMEM((2 * share * subs, total), bf16),
             pltpu.VMEM((2 * share, total), f32),
             pltpu.VMEM((2 * share, total), f32),

time: 33.7 us -> 32.6 us (0.967)
  Pallas kernels: 8.59 us -> 7.51 us
    pallas_call x1, Pallas kernels: 6.29 us -> 5.2 us  [by_beams(): pl.pallas_call(functools.partial(beam_kernel, counts, beams, math.sqrt(al...]
where the time goes in v4:
time: 32.6 us; the launch traced here: 32.3 us
  blocking collectives  24.2 us (74%)
  Pallas kernels  7.51 us (23%)
  between operations  0.65 us (2%)
    all_to_all x2, blocking collectives, exchange(): lax.all_to_all(cut, ('row', 'col'), 0, 0, tiled=False).reshape(x.shape)  24.2 us
    pallas_call x1, Pallas kernels, by_beams(): pl.pallas_call(functools.partial(beam_kernel, counts, beams, math.sqrt(al...  5.2 us
    pallas_call x1, Pallas kernels, by_beams(): pl.pallas_call(functools.partial(split_kernel, counts, beams, elems), in_...  1.18 us
    pallas_call x1, Pallas kernels, by_beams(): pl.pallas_call(functools.partial(join_kernel, ranks, beams, elems), out_s...  1.12 us

profile of v4, /device:TPU:0, one launch (start us, length us, event | category | flops | bytes accessed | tf_op | source)
XLA Modules:
  0.0 32.3 jit_solution(10276842514513438689)
XLA Ops:
  0.6 1.2 %shard_map.68 = (bf16[384,128]{1,0:T(8,128)(2,1)S(1)}, bf16[32,64,128]{2,1,0:T(8,128)(2,1)S(1)}, f32[2,2048]{1,0:T(2,128)S(1)}, s32[8,128]{1,0:T(8,128)S(1)}) custom-call(f32[2,2,2,2048]{3,2,1,0:T(2,128)} %currents.1, s32[2,2,25]{2,1,0:T(2,128)} %ids_far.1, bf16[32,64,128]{2,1,0:T(8,128)(2,1)} %library_far.1, f32[2,2048]{1,0:T(2,128)} %dirs_far.1, ...), custom_call_target="tpu_custom_call" | custom-call | tf_op jit(solution)/shard_map/pallas_call | solution.py:624
  1.8 14.6 %all_to_all.10 = bf16[16,24,128]{2,1,0:T(8,128)(2,1)S(1)} all-to-all(bf16[16,24,128]{2,1,0:T(8,128)(2,1)S(1)} %bitcast.8), channel_id=1, replica_groups=mesh['groups'=2,'row'=4,'col'=4] {'row','col'}, dimensions={0} | all-to-all | bytes 196608 | tf_op jit(solution)/shard_map/all_to_all | solution.py:622
  16.4 5.2 %shard_map.69 = bf16[256,128]{1,0:T(8,128)(2,1)S(1)} custom-call(bf16[384,128]{1,0:T(8,128)(2,1)S(1)} %bitcast.5, bf16[32,64,128]{2,1,0:T(8,128)(2,1)S(1)} %get-tuple-element.9.library, f32[2,2048]{1,0:T(2,128)S(1)} %get-tuple-element.10.dirs, s32[8,128]{1,0:T(8,128)S(1)} %get-tuple-element.11.aims), custom_call_target="tpu_custom_call" | custom-call | tf_op jit(solution)/shard_map/pallas_call | solution.py:642
  21.6 0.0 copy-start
  21.6 9.6 %all_to_all.11 = bf16[16,16,128]{2,1,0:T(8,128)(2,1)S(1)} all-to-all(bf16[16,16,128]{2,1,0:T(8,128)(2,1)S(1)} %bitcast.7), channel_id=1, replica_groups=mesh['groups'=2,'row'=4,'col'=4] {'row','col'}, dimensions={0} | all-to-all | bytes 131072 | tf_op jit(solution)/shard_map/all_to_all | solution.py:622
  31.2 0.0 copy-done
  31.2 1.1 %shard_map.70 = (f32[2,2,2,2048]{3,2,1,0:T(2,128)}, f32[64,128]{1,0:T(8,128)}) custom-call(f32[2,2,2,2048]{3,2,1,0:T(2,128)S(1)} %copy-done, bf16[256,128]{1,0:T(8,128)(2,1)S(1)} %bitcast.6), custom_call_target="tpu_custom_call" | custom-call | tf_op jit(solution)/shard_map/pallas_call | solution.py:669
Async XLA Ops:
  21.6 9.6 %copy-start = (f32[2,2,2,2048]{3,2,1,0:T(2,128)S(1)}, f32[2,2,2,2048]{3,2,1,0:T(2,128)}, u32[]{:S(2)}) copy-start(f32[2,2,2,2048]{3,2,1,0:T(2,128)} %currents.1) | copy-start | bytes 196612

commit v5 on v4

--- a/solution.py
+++ b/solution.py
@@ -284,7 +284,7 @@
 
 def split_kernel(
     counts, beams, elems, currents_far, ids_far, library_far, dirs_far, beam_dir_far,
-    out, library, dirs, aims, currents, ids, beam_dir, work, arrived,
+    out, library, dirs, aims, order, currents, ids, beam_dir, work, arrived,
 ):
     ranks = counts[0] * counts[1]
     me = lax.axis_index("row") * counts[1] + lax.axis_index("col")
@@ -305,7 +305,7 @@
     _, rows, cols, packed = currents.shape
     places = rows * cols
     groups = lanes // beams
-    order = shuffle(elems, places)
+    order[...] = shuffle(elems, places)
     for copy in copies[:2]:
         copy.wait()
     field = jnp.concatenate([currents[a, b] for a in range(2) for b in range(rows)], axis=0)
@@ -321,7 +321,7 @@
         ],
         axis=0,
     )
-    moved = jnp.dot(stacked, order, preferred_element_type=jnp.float32)
+    moved = jnp.dot(stacked, order[...], preferred_element_type=jnp.float32)
     share = beams // ranks
     kept = share * places
     for half in range(2):
@@ -332,12 +332,27 @@
                 work[pl.ds(row, ranks, stride=message), :] = moved[
                     first : first + ranks, p * lanes : (p + 1) * lanes
                 ]
-    slots = ids.shape[2]
-    table = jnp.concatenate([ids[a] for a in range(rows)], axis=0).astype(jnp.float32)
-    table = jnp.concatenate([table, jnp.zeros((places, lanes - slots), jnp.float32)], axis=1)
-    table = jnp.concatenate([table, jnp.zeros_like(table)], axis=0)
+    table = jnp.concatenate([ids[a] for a in range(rows)], axis=0)
+    table = jnp.concatenate([table, table], axis=0)
+    o = iota((2 * places, 1), 0) % places
+    subs = ranks * places
+    t = iota((1, lanes), 1) % subs
+    t_place, t_rank = t // ranks, t % ranks
+    t_row = (t_rank // counts[1]) * rows + t_place // cols
+    t_col = (t_rank % counts[1]) * cols + t_place % cols
+    row_gap = t_row - (lax.axis_index("row") * rows + o // cols)
+    col_gap = t_col - (lax.axis_index("col") * cols + o % cols)
+    gap = row_gap * 64 + col_gap
+    pair = jnp.full((2 * places, lanes), -1, jnp.int32)
+    for row_off in range(5):
+        for col_off in range(5):
+            slot = 5 * row_off + col_off
+            pair = jnp.where(
+                gap == (row_off - 2) * 64 + (col_off - 2), table[:, slot : slot + 1], pair
+            )
+    pair = pair.astype(jnp.float32)
     for m in range(ranks):
-        work[m * message + 2 * kept : (m + 1) * message, :] = table
+        work[m * message + 2 * kept : (m + 1) * message, :] = pair
     out[...] = work[...].astype(jnp.bfloat16)
     for copy in copies[2:]:
         copy.wait()
@@ -348,7 +363,7 @@
     aims[...] = aim
 
 
-def join_kernel(ranks, beams, elems, currents, moved_in, new_currents, far, work):
+def join_kernel(ranks, beams, currents, moved_in, order, new_currents, far, work):
     _, rows, cols, packed = currents.shape
     places = rows * cols
     groups = lanes // beams
@@ -367,7 +382,7 @@
     ).astype(jnp.bfloat16)
     back = lax.dot_general(
         stacked,
-        shuffle(elems, places),
+        order[...],
         (((1,), (1,)), ((), ())),
         preferred_element_type=jnp.float32,
     )
@@ -405,40 +420,21 @@
     field_rows = share * subs
     real_lane = iota((1, lanes), 1) < elems
 
-    s = iota((subs, 1), 0)
-    place, rank = s // ranks, s % ranks
-    sub_row = (rank // col_count) * place_rows + place // place_cols
-    sub_col = (rank % col_count) * place_cols + place % place_cols
     def received(first):
         return opened[pl.ds(first, ranks, stride=message), :]
 
     opened[...] = given[...].astype(jnp.float32)
     kept = share * places
     field = jnp.concatenate([received(i) + received(kept + i) for i in range(kept)], axis=0)
-    ids = jnp.concatenate([received(2 * kept + p) for p in range(places)], axis=0)
-    ids = ids.astype(jnp.int32)
-
-    code = sub_row * 64 + sub_col
-    t = iota((1, subs), 1)
-    t_place, t_rank = t // ranks, t % ranks
-    t_row = (t_rank // col_count) * place_rows + t_place // place_cols
-    t_col = (t_rank % col_count) * place_cols + t_place % place_cols
-    gap = t_row * 64 + t_col - code
-    pair = jnp.full((subs, subs), -1, jnp.int32)
-    for row_off in range(5):
-        for col_off in range(5):
-            slot = 5 * row_off + col_off
-            pair = jnp.where(
-                gap == (row_off - 2) * 64 + (col_off - 2), ids[:, slot : slot + 1], pair
-            )
-    pair_adjoint = pair.astype(jnp.float32).T.astype(jnp.int32)
+    pair = jnp.concatenate([received(2 * kept + p) for p in range(places)], axis=0)
+    adjoint = pair[:, :subs].T
+    pair_adjoint = jnp.concatenate([adjoint, adjoint], axis=1)
 
     def choose(goal, table):
-        twice = jnp.concatenate([table, table], axis=1)
-        value = iota((1, 2 * subs), 1) // subs
+        value = (iota((1, 2 * subs), 1) // subs).astype(jnp.float32)
         for v in range(0, values, 2):
             goal[:, v * subs : (v + 2) * subs] = (
-                (twice == value + v).astype(jnp.float32).astype(jnp.bfloat16)
+                (table == value + v).astype(jnp.float32).astype(jnp.bfloat16)
             )
 
     choose(chosen, pair)
@@ -603,7 +599,7 @@
 
 def by_beams(currents, library, block_ids, dirs, beam_dir):
     beams = beam_dir.shape[0]
-    _, rows_here, cols_here, _ = currents.shape
+    _, rows_here, cols_here, packed = currents.shape
     values, elems, _ = library.shape
     counts = (lax.axis_size("row"), lax.axis_size("col"))
     ranks = counts[0] * counts[1]
@@ -612,7 +608,7 @@
     all_elems = subs * elems
     total = dirs.shape[1]
     f32, bf16 = jnp.float32, jnp.bfloat16
-    params = pltpu.CompilerParams(vmem_limit_bytes=40 * 2**20)
+    params = pltpu.CompilerParams(vmem_limit_bytes=24 * 2**20)
 
     def keep(x):
         return pltpu.with_memory_space_constraint(x, pltpu.HBM)
@@ -621,7 +617,7 @@
         cut = x.reshape(ranks, -1, lanes)
         return lax.all_to_all(cut, ("row", "col"), 0, 0, tiled=False).reshape(x.shape)
 
-    sent, library_near, dirs_near, aims = pl.pallas_call(
+    sent, library_near, dirs_near, aims, order = pl.pallas_call(
         functools.partial(split_kernel, counts, beams, elems),
         in_specs=[pl.BlockSpec(memory_space=pltpu.HBM)] * 5,
         out_shape=(
@@ -629,6 +625,7 @@
             jax.ShapeDtypeStruct(library.shape, bf16),
             jax.ShapeDtypeStruct(dirs.shape, f32),
             jax.ShapeDtypeStruct((8, lanes), jnp.int32),
+            jax.ShapeDtypeStruct((2 * packed // beams * rows_here * cols_here,) * 2, bf16),
         ),
         scratch_shapes=[
             pltpu.VMEM(currents.shape, f32),
@@ -667,14 +664,14 @@
         compiler_params=params,
     )(exchange(sent), library_near, dirs_near, aims)
     new_currents, far = pl.pallas_call(
-        functools.partial(join_kernel, ranks, beams, elems),
+        functools.partial(join_kernel, ranks, beams),
         out_shape=(
             jax.ShapeDtypeStruct(currents.shape, f32),
             jax.ShapeDtypeStruct((2 * beams, total // ranks), f32),
         ),
         scratch_shapes=[pltpu.VMEM((16 * ranks, lanes), f32)],
         compiler_params=params,
-    )(currents, exchange(results))
+    )(currents, exchange(results), order)
     return new_currents, far.T
 
 

time: 32.6 us -> 32.1 us (0.985)
  Pallas kernels: 7.51 us -> 7.07 us
where the time goes in v5:
time: 32.1 us; the launch traced here: 31.9 us
  blocking collectives  24.2 us (75%)
  Pallas kernels  7.07 us (22%)
  between operations  0.65 us (2%)
    all_to_all x2, blocking collectives, exchange(): lax.all_to_all(cut, ('row', 'col'), 0, 0, tiled=False).reshape(x.shape)  24.2 us
    pallas_call x1, Pallas kernels, by_beams(): pl.pallas_call(functools.partial(beam_kernel, counts, beams, math.sqrt(al...  4.88 us
    pallas_call x1, Pallas kernels, by_beams(): pl.pallas_call(functools.partial(split_kernel, counts, beams, elems), in_...  1.18 us
    pallas_call x1, Pallas kernels, by_beams(): pl.pallas_call(functools.partial(join_kernel, ranks, beams), out_shape=(j...  1 us

profile of v5, /device:TPU:0, one launch (start us, length us, event | category | flops | bytes accessed | tf_op | source)
XLA Modules:
  0.0 31.9 jit_solution(15994235832551043944)
XLA Ops:
  0.6 1.2 %shard_map.68 = (bf16[384,128]{1,0:T(8,128)(2,1)S(1)}, bf16[32,64,128]{2,1,0:T(8,128)(2,1)S(1)}, f32[2,2048]{1,0:T(2,128)S(1)}, s32[8,128]{1,0:T(8,128)S(1)}, bf16[512,512]{1,0:T(8,128)(2,1)S(1)}) custom-call(f32[2,2,2,2048]{3,2,1,0:T(2,128)} %currents.1, s32[2,2,25]{2,1,0:T(2,128)} %ids_far.1, bf16[32,64,128]{2,1,0:T(8,128)(2,1)} %library_far.1, ...), custom_call_target="tpu_custom_call" | custom-call | tf_op jit(solution)/shard_map/pallas_call | solution.py:620
  1.8 14.6 %all_to_all.10 = bf16[16,24,128]{2,1,0:T(8,128)(2,1)S(1)} all-to-all(bf16[16,24,128]{2,1,0:T(8,128)(2,1)S(1)} %bitcast.8), channel_id=1, replica_groups=mesh['groups'=2,'row'=4,'col'=4] {'row','col'}, dimensions={0} | all-to-all | bytes 196608 | tf_op jit(solution)/shard_map/all_to_all | solution.py:618
  16.4 4.9 %shard_map.69 = bf16[256,128]{1,0:T(8,128)(2,1)S(1)} custom-call(bf16[384,128]{1,0:T(8,128)(2,1)S(1)} %bitcast.5, bf16[32,64,128]{2,1,0:T(8,128)(2,1)S(1)} %get-tuple-element.10.library, f32[2,2048]{1,0:T(2,128)S(1)} %get-tuple-element.11.dirs, s32[8,128]{1,0:T(8,128)S(1)} %get-tuple-element.12.aims), custom_call_target="tpu_custom_call" | custom-call | tf_op jit(solution)/shard_map/pallas_call | solution.py:639
  21.3 0.0 copy-start
  21.3 9.6 %all_to_all.11 = bf16[16,16,128]{2,1,0:T(8,128)(2,1)S(1)} all-to-all(bf16[16,16,128]{2,1,0:T(8,128)(2,1)S(1)} %bitcast.7), channel_id=1, replica_groups=mesh['groups'=2,'row'=4,'col'=4] {'row','col'}, dimensions={0} | all-to-all | bytes 131072 | tf_op jit(solution)/shard_map/all_to_all | solution.py:618
  30.9 0.0 copy-done
  30.9 1.0 %shard_map.70 = (f32[2,2,2,2048]{3,2,1,0:T(2,128)}, f32[64,128]{1,0:T(8,128)}) custom-call(f32[2,2,2,2048]{3,2,1,0:T(2,128)S(1)} %copy-done, bf16[256,128]{1,0:T(8,128)(2,1)S(1)} %bitcast.6, bf16[512,512]{1,0:T(8,128)(2,1)S(1)} %get-tuple-element.13.order), custom_call_target="tpu_custom_call" | custom-call | tf_op jit(solution)/shard_map/pallas_call | solution.py:666
Async XLA Ops:
  21.3 9.6 %copy-start = (f32[2,2,2,2048]{3,2,1,0:T(2,128)S(1)}, f32[2,2,2,2048]{3,2,1,0:T(2,128)}, u32[]{:S(2)}) copy-start(f32[2,2,2,2048]{3,2,1,0:T(2,128)} %currents.1) | copy-start | bytes 196612

commit v6 on v5

--- a/solution.py
+++ b/solution.py
@@ -287,7 +287,7 @@
     out, library, dirs, aims, order, currents, ids, beam_dir, work, arrived,
 ):
     ranks = counts[0] * counts[1]
-    me = lax.axis_index("row") * counts[1] + lax.axis_index("col")
+    me = lax.axis_index("col") * counts[0] + lax.axis_index("row")
     copies = [
         pltpu.make_async_copy(source, goal, arrived.at[i])
         for i, (source, goal) in enumerate(
@@ -338,8 +338,8 @@
     subs = ranks * places
     t = iota((1, lanes), 1) % subs
     t_place, t_rank = t // ranks, t % ranks
-    t_row = (t_rank // counts[1]) * rows + t_place // cols
-    t_col = (t_rank % counts[1]) * cols + t_place % cols
+    t_row = (t_rank % counts[0]) * rows + t_place // cols
+    t_col = (t_rank // counts[0]) * cols + t_place % cols
     row_gap = t_row - (lax.axis_index("row") * rows + o // cols)
     col_gap = t_col - (lax.axis_index("col") * cols + o % cols)
     gap = row_gap * 64 + col_gap
@@ -459,17 +459,17 @@
         for p in range(places):
             x0 = (p % place_cols) * col_count
             y0 = (p // place_cols) * row_count
-            xs = [jnp.concatenate([t[x0 : x0 + col_count]] * row_count, axis=0) for t in x_turn]
-            ys = [
+            xs = [
                 jnp.concatenate(
                     [
-                        jnp.broadcast_to(t[y0 + k : y0 + k + 1], (col_count, chunk))
-                        for k in range(row_count)
+                        jnp.broadcast_to(t[x0 + k : x0 + k + 1], (row_count, chunk))
+                        for k in range(col_count)
                     ],
                     axis=0,
                 )
-                for t in y_turn
+                for t in x_turn
             ]
+            ys = [jnp.concatenate([t[y0 : y0 + row_count]] * col_count, axis=0) for t in y_turn]
             cosine, sine = multiply(xs, ys)
             sub_re[p * ranks : (p + 1) * ranks, cut] = cosine
             sub_im[p * ranks : (p + 1) * ranks, cut] = -sine
@@ -593,7 +593,8 @@
     both = jnp.concatenate([high, final - high], axis=0)
     piece = total // ranks
     for m in range(ranks):
-        work[m * 16 + 8 : m * 16 + 16, :] = both[:, m * piece : (m + 1) * piece]
+        owner = (m % row_count) * col_count + m // row_count
+        work[m * 16 + 8 : m * 16 + 16, :] = both[:, owner * piece : (owner + 1) * piece]
     out[...] = work[...].astype(jnp.bfloat16)
 
 
@@ -615,7 +616,7 @@
 
     def exchange(x):
         cut = x.reshape(ranks, -1, lanes)
-        return lax.all_to_all(cut, ("row", "col"), 0, 0, tiled=False).reshape(x.shape)
+        return lax.all_to_all(cut, ("col", "row"), 0, 0, tiled=False).reshape(x.shape)
 
     sent, library_near, dirs_near, aims, order = pl.pallas_call(
         functools.partial(split_kernel, counts, beams, elems),

time: 32.1 us -> 31.6 us (0.984)
  blocking collectives: 24.2 us -> 23.6 us
    all_to_all x2, blocking collectives: 24.2 us -> 23.6 us  [exchange(): lax.all_to_all(cut, ('col', 'row'), 0, 0, tiled=False).reshape(x.shape)]
where the time goes in v6:
time: 31.6 us; the launch traced here: 31.3 us
  blocking collectives  23.6 us (75%)
  Pallas kernels  7.07 us (22%)
  between operations  0.65 us (2%)
    all_to_all x2, blocking collectives, exchange(): lax.all_to_all(cut, ('col', 'row'), 0, 0, tiled=False).reshape(x.shape)  23.6 us
    pallas_call x1, Pallas kernels, by_beams(): pl.pallas_call(functools.partial(beam_kernel, counts, beams, math.sqrt(al...  4.89 us
    pallas_call x1, Pallas kernels, by_beams(): pl.pallas_call(functools.partial(split_kernel, counts, beams, elems), in_...  1.18 us
    pallas_call x1, Pallas kernels, by_beams(): pl.pallas_call(functools.partial(join_kernel, ranks, beams), out_shape=(j...  1 us

profile of v6, /device:TPU:0, one launch (start us, length us, event | category | flops | bytes accessed | tf_op | source)
XLA Modules:
  0.0 31.3 jit_solution(6357077775063581288)
XLA Ops:
  0.6 1.2 %shard_map.68 = (bf16[384,128]{1,0:T(8,128)(2,1)S(1)}, bf16[32,64,128]{2,1,0:T(8,128)(2,1)S(1)}, f32[2,2048]{1,0:T(2,128)S(1)}, s32[8,128]{1,0:T(8,128)S(1)}, bf16[512,512]{1,0:T(8,128)(2,1)S(1)}) custom-call(f32[2,2,2,2048]{3,2,1,0:T(2,128)} %currents.1, s32[2,2,25]{2,1,0:T(2,128)} %ids_far.1, bf16[32,64,128]{2,1,0:T(8,128)(2,1)} %library_far.1, ...), custom_call_target="tpu_custom_call" | custom-call | tf_op jit(solution)/shard_map/pallas_call | solution.py:621
  1.8 14.2 %all_to_all.10 = bf16[16,24,128]{2,1,0:T(8,128)(2,1)S(1)} all-to-all(bf16[16,24,128]{2,1,0:T(8,128)(2,1)S(1)} %bitcast.8), channel_id=1, replica_groups=mesh['groups'=2,'row'=4,'col'=4] {'col','row'}, dimensions={0} | all-to-all | bytes 196608 | tf_op jit(solution)/shard_map/all_to_all | solution.py:619
  16.0 4.9 %shard_map.69 = bf16[256,128]{1,0:T(8,128)(2,1)S(1)} custom-call(bf16[384,128]{1,0:T(8,128)(2,1)S(1)} %bitcast.5, bf16[32,64,128]{2,1,0:T(8,128)(2,1)S(1)} %get-tuple-element.10.library, f32[2,2048]{1,0:T(2,128)S(1)} %get-tuple-element.11.dirs, s32[8,128]{1,0:T(8,128)S(1)} %get-tuple-element.12.aims), custom_call_target="tpu_custom_call" | custom-call | tf_op jit(solution)/shard_map/pallas_call | solution.py:640
  20.9 0.0 copy-start
  20.9 9.4 %all_to_all.11 = bf16[16,16,128]{2,1,0:T(8,128)(2,1)S(1)} all-to-all(bf16[16,16,128]{2,1,0:T(8,128)(2,1)S(1)} %bitcast.7), channel_id=1, replica_groups=mesh['groups'=2,'row'=4,'col'=4] {'col','row'}, dimensions={0} | all-to-all | bytes 131072 | tf_op jit(solution)/shard_map/all_to_all | solution.py:619
  30.3 0.0 copy-done
  30.3 1.0 %shard_map.70 = (f32[2,2,2,2048]{3,2,1,0:T(2,128)}, f32[64,128]{1,0:T(8,128)}) custom-call(f32[2,2,2,2048]{3,2,1,0:T(2,128)S(1)} %copy-done, bf16[256,128]{1,0:T(8,128)(2,1)S(1)} %bitcast.6, bf16[512,512]{1,0:T(8,128)(2,1)S(1)} %get-tuple-element.13.order), custom_call_target="tpu_custom_call" | custom-call | tf_op jit(solution)/shard_map/pallas_call | solution.py:667
Async XLA Ops:
  20.9 9.4 %copy-start = (f32[2,2,2,2048]{3,2,1,0:T(2,128)S(1)}, f32[2,2,2,2048]{3,2,1,0:T(2,128)}, u32[]{:S(2)}) copy-start(f32[2,2,2,2048]{3,2,1,0:T(2,128)} %currents.1) | copy-start | bytes 196612

commit v7 on v6

--- a/solution.py
+++ b/solution.py
@@ -247,6 +247,7 @@
 lanes = 128
 chunk = 256
 message = 24
+span = 4
 sin_fit = (3.141592580044754, -5.167706878916943, 2.5500313770294833, -0.5980451722529145, 0.07722012475690251)
 cos_fit = (0.9999999535196061, -4.934792861473954, 4.058411954029988, -1.3318803713197287, 0.21969716737372766)
 
@@ -363,7 +364,9 @@
     aims[...] = aim
 
 
-def join_kernel(ranks, beams, currents, moved_in, order, new_currents, far, work):
+def join_kernel(
+    ranks, beams, currents, moved_in, order, new_currents_out, far_out, work, new_currents, far, gone
+):
     _, rows, cols, packed = currents.shape
     places = rows * cols
     groups = lanes // beams
@@ -373,6 +376,12 @@
     def rows_of(first):
         return work[pl.ds(first, ranks, stride=16), :]
 
+    pattern = jnp.concatenate(
+        [rows_of(8 + i) + rows_of(8 + 2 * share + i) for i in range(2 * share)], axis=0
+    )
+    far[...] = pattern
+    sent_far = pltpu.make_async_copy(far, far_out, gone.at[0])
+    sent_far.start()
     stacked = jnp.concatenate(
         [
             jnp.concatenate([rows_of(bl * places + p) for p in range(places)], axis=1)
@@ -395,10 +404,10 @@
         for b in range(rows):
             first = (a * rows + b) * cols
             new_currents[a, b] = currents[a, b] - moved[first : first + cols]
-    pattern = jnp.concatenate(
-        [rows_of(8 + i) + rows_of(8 + 2 * share + i) for i in range(2 * share)], axis=0
-    )
-    far[...] = pattern
+    sent_currents = pltpu.make_async_copy(new_currents, new_currents_out, gone.at[1])
+    sent_currents.start()
+    sent_far.wait()
+    sent_currents.wait()
 
 
 def beam_kernel(
@@ -533,8 +542,7 @@
         both = jnp.concatenate([real, swap(total_field)], axis=0).astype(jnp.bfloat16)
         return jnp.concatenate([both, both], axis=1)
 
-    def project(radiated, cut):
-        part = jnp.dot(radiated, off[:, cut], preferred_element_type=jnp.float32)
+    def project(part, cut):
         s_re, s_im = sub_re[:, cut], sub_im[:, cut]
         re, im = [], []
         for bl in range(share):
@@ -548,7 +556,13 @@
     place = aims[0 : 2 * share, 0:1]
     for i in range(chunks):
         cut = slice(i * chunk, (i + 1) * chunk)
-        found = project(radiated, cut)
+        if i % span == 0:
+            parts = jnp.dot(
+                radiated,
+                off[:, i * chunk : (i + span) * chunk],
+                preferred_element_type=jnp.float32,
+            )
+        found = project(parts[:, (i % span) * chunk : (i % span + 1) * chunk], cut)
         pattern[:, cut] = found
         rest = found - jnp.where(iota((1, chunk), 1) + i * chunk == place, amplitude, 0.0)
         residual[:, cut] = rest
@@ -575,7 +589,13 @@
     squares = jnp.zeros((2 * share, chunk), jnp.float32)
     for i in range(chunks):
         cut = slice(i * chunk, (i + 1) * chunk)
-        found = project(radiated, cut)
+        if i % span == 0:
+            parts = jnp.dot(
+                radiated,
+                off[:, i * chunk : (i + span) * chunk],
+                preferred_element_type=jnp.float32,
+            )
+        found = project(parts[:, (i % span) * chunk : (i % span + 1) * chunk], cut)
         image[:, cut] = found
         products = products + found * residual[:, cut]
         squares = squares + found * found
@@ -670,7 +690,13 @@
             jax.ShapeDtypeStruct(currents.shape, f32),
             jax.ShapeDtypeStruct((2 * beams, total // ranks), f32),
         ),
-        scratch_shapes=[pltpu.VMEM((16 * ranks, lanes), f32)],
+        out_specs=[pl.BlockSpec(memory_space=pltpu.HBM)] * 2,
+        scratch_shapes=[
+            pltpu.VMEM((16 * ranks, lanes), f32),
+            pltpu.VMEM(currents.shape, f32),
+            pltpu.VMEM((2 * beams, total // ranks), f32),
+            pltpu.SemaphoreType.DMA((2,)),
+        ],
         compiler_params=params,
     )(currents, exchange(results), order)
     return new_currents, far.T

time: 31.6 us -> 31.6 us (level)
  no operation moved by 1% of the time
where the time goes in v7:
time: 31.6 us; the launch traced here: 31.3 us
  blocking collectives  23.6 us (75%)
  Pallas kernels  7.09 us (22%)
  between operations  0.65 us (2%)
    all_to_all x2, blocking collectives, exchange(): lax.all_to_all(cut, ('col', 'row'), 0, 0, tiled=False).reshape(x.shape)  23.6 us
    pallas_call x1, Pallas kernels, by_beams(): pl.pallas_call(functools.partial(beam_kernel, counts, beams, math.sqrt(al...  4.89 us
    pallas_call x1, Pallas kernels, by_beams(): pl.pallas_call(functools.partial(split_kernel, counts, beams, elems), in_...  1.18 us
    pallas_call x1, Pallas kernels, by_beams(): pl.pallas_call(functools.partial(join_kernel, ranks, beams), out_shape=(j...  1.02 us

profile of v7, /device:TPU:0, one launch (start us, length us, event | category | flops | bytes accessed | tf_op | source)
XLA Modules:
  0.0 31.3 jit_solution(1549932911908467517)
XLA Ops:
  0.6 1.2 %shard_map.68 = (bf16[384,128]{1,0:T(8,128)(2,1)S(1)}, bf16[32,64,128]{2,1,0:T(8,128)(2,1)S(1)}, f32[2,2048]{1,0:T(2,128)S(1)}, s32[8,128]{1,0:T(8,128)S(1)}, bf16[512,512]{1,0:T(8,128)(2,1)S(1)}) custom-call(f32[2,2,2,2048]{3,2,1,0:T(2,128)} %currents.1, s32[2,2,25]{2,1,0:T(2,128)} %ids_far.1, bf16[32,64,128]{2,1,0:T(8,128)(2,1)} %library_far.1, ...), custom_call_target="tpu_custom_call" | custom-call | tf_op jit(solution)/shard_map/pallas_call | solution.py:641
  1.8 14.2 %all_to_all.10 = bf16[16,24,128]{2,1,0:T(8,128)(2,1)S(1)} all-to-all(bf16[16,24,128]{2,1,0:T(8,128)(2,1)S(1)} %bitcast.8), channel_id=1, replica_groups=mesh['groups'=2,'row'=4,'col'=4] {'col','row'}, dimensions={0} | all-to-all | bytes 196608 | tf_op jit(solution)/shard_map/all_to_all | solution.py:639
  16.0 4.9 %shard_map.69 = bf16[256,128]{1,0:T(8,128)(2,1)S(1)} custom-call(bf16[384,128]{1,0:T(8,128)(2,1)S(1)} %bitcast.5, bf16[32,64,128]{2,1,0:T(8,128)(2,1)S(1)} %get-tuple-element.10.library, f32[2,2048]{1,0:T(2,128)S(1)} %get-tuple-element.11.dirs, s32[8,128]{1,0:T(8,128)S(1)} %get-tuple-element.12.aims), custom_call_target="tpu_custom_call" | custom-call | tf_op jit(solution)/shard_map/pallas_call | solution.py:660
  20.9 0.0 copy-start
  20.9 9.4 %all_to_all.11 = bf16[16,16,128]{2,1,0:T(8,128)(2,1)S(1)} all-to-all(bf16[16,16,128]{2,1,0:T(8,128)(2,1)S(1)} %bitcast.7), channel_id=1, replica_groups=mesh['groups'=2,'row'=4,'col'=4] {'col','row'}, dimensions={0} | all-to-all | bytes 131072 | tf_op jit(solution)/shard_map/all_to_all | solution.py:639
  30.3 0.0 copy-done
  30.3 1.0 %shard_map.70 = (f32[2,2,2,2048]{3,2,1,0:T(2,128)}, f32[64,128]{1,0:T(8,128)}) custom-call(f32[2,2,2,2048]{3,2,1,0:T(2,128)S(1)} %copy-done, bf16[256,128]{1,0:T(8,128)(2,1)S(1)} %bitcast.6, bf16[512,512]{1,0:T(8,128)(2,1)S(1)} %get-tuple-element.13.order), custom_call_target="tpu_custom_call" | custom-call | tf_op jit(solution)/shard_map/pallas_call | solution.py:687
Async XLA Ops:
  20.9 9.4 %copy-start = (f32[2,2,2,2048]{3,2,1,0:T(2,128)S(1)}, f32[2,2,2,2048]{3,2,1,0:T(2,128)}, u32[]{:S(2)}) copy-start(f32[2,2,2,2048]{3,2,1,0:T(2,128)} %currents.1) | copy-start | bytes 196612
